TPU v7x, 512 devices: a whole 4x8x8 slice. The times are simulated.
512 devices in a mesh: dp: 16 (over y_hi, x), tensor: 32 (over z, y_lo, core).
Axes of the slice: x: 4, y: 8 (y_hi: 4, y_lo: 2; y = y_hi * 2 + y_lo), z: 8, core: 2. Of those that a mesh axis runs over, the one named last changes fastest.
Arguments:
- grad_a_parts: float32 [16, 512, 4096], P('dp', None, 'tensor'), may hold values from -0.125 to 0.125
- grad_b_parts: float32 [16, 12288, 32], P('dp', 'tensor'), may hold values from -0.125 to 0.125
- factor_a: float32 [512, 4096], P('dp', 'tensor'), may hold values from -0.25 to 0.25
- moment_a: float32 [512, 4096], P('dp', 'tensor'), may hold values from -0.25 to 0.25
- factor_b: float32 [12288, 32], P(('tensor', 'dp')), may hold values from -0.25 to 0.25
- moment_b: float32 [12288, 32], P(('tensor', 'dp')), may hold values from -0.25 to 0.25
- base_down: bfloat16 [12288, 4096], P('tensor'), may hold values from -0.21875 to 0.21875
- slot_hidden: bfloat16 [3072, 12288], P('dp', 'tensor'), may hold values from -6 to 6
- expert_ids: int32 [4096, 8], P('dp'), may hold values from 0 to 15, all different within a row; in each aligned block of 256 rows (0 to 255, 256 to 511, ...) at most 192 rows name the same one
- combine_weights: float32 [4096, 8], P('dp'), may hold values from 0.05 to 0.5
Outputs:
- stepped_factor_a: float32 [512, 4096], P('dp', 'tensor')
- stepped_factor_b: float32 [12288, 32], P(('tensor', 'dp'))
- scored: bfloat16 [4096, 4096], P(('dp', 'tensor'))
Inputs may be any that keep to these rules, and one draw needn't show every extreme that they name: `expert_ids`: within each replica group's 256 tokens no expert is chosen more than 192 times, a bound that some block reaches; slots of an expert past its count in a group are never read.
All inputs are finite; a program needn't handle non-finite values.
Results may differ from a plain program's by a relative error of at most 0.0054.
Values may be sent and summed in bfloat16 or wider, within the bound.
No kernel may reach another device: no remote copies, remote signals or barrier semaphores. Data moves between devices by JAX's collectives and lax.ppermute only.
A program may use at most 64 MiB of HBM per device.

v0:
```python
import jax
import jax.numpy as jnp
from jax import lax
from jax.sharding import PartitionSpec as P

HALF_HIDDEN = 768
ADAPTER_RANK = 32
EXPERTS = 16


MOMENTUM = 0.9
RATE = 0.5


def slot_positions(expert_ids):
    flat = expert_ids.reshape(-1)
    onehot = (flat[:, None] == jnp.arange(EXPERTS, dtype=jnp.int32)[None, :]).astype(jnp.int32)
    before = jnp.cumsum(onehot, axis=0) - onehot
    return jnp.sum(before * onehot, axis=1).reshape(expert_ids.shape)


def combine_table(expert_ids, slots, weights, expert_index, slot_count):
    columns = jnp.arange(slot_count, dtype=jnp.int32)
    hit = (expert_ids == expert_index)[:, :, None] & (slots[:, :, None] == columns[None, None, :])
    return jnp.sum(jnp.where(hit, weights[:, :, None], jnp.zeros((), weights.dtype)), axis=1)


def body(
    grad_a_parts,
    grad_b_parts,
    factor_a,
    moment_a,
    factor_b,
    moment_b,
    base_down,
    slot_hidden,
    expert_ids,
    combine_weights,
):
    hid_rows = base_down.shape[0]
    width = base_down.shape[1]
    slot_count = slot_hidden.shape[0]
    tok_group = expert_ids.shape[0]
    grad_a, grad_b = (
        lax.psum_scatter(grad_a_parts[0], "dp", scatter_dimension=0, tiled=True),
        lax.psum_scatter(grad_b_parts[0], "dp", scatter_dimension=0, tiled=True),
    )
    stepped_factor_a = factor_a - RATE * (MOMENTUM * moment_a + grad_a)
    stepped_factor_b = factor_b - RATE * (MOMENTUM * moment_b + grad_b)
    wide_a = lax.all_gather(stepped_factor_a.astype(jnp.bfloat16), "tensor", axis=1, tiled=True)
    local_count = max(1, hid_rows // HALF_HIDDEN)
    local_width = min(hid_rows, HALF_HIDDEN)
    first = lax.axis_index("tensor") * hid_rows // HALF_HIDDEN
    every = lax.all_gather(wide_a, "dp", axis=0, tiled=True)
    mine = lax.dynamic_slice_in_dim(every, first * ADAPTER_RANK, local_count * ADAPTER_RANK, 0)
    rows_b = lax.all_gather(stepped_factor_b.astype(jnp.bfloat16), "dp", axis=0, tiled=True)
    factors_b = rows_b.reshape(local_count, local_width, ADAPTER_RANK)
    factors_a = mine.reshape(local_count, ADAPTER_RANK, width)
    update = jnp.einsum("efr,erd->efd", factors_b, factors_a, preferred_element_type=jnp.float32)
    merged = (
        base_down.reshape(local_count, local_width, width).astype(jnp.float32) + update
    ).astype(jnp.bfloat16)
    hidden = slot_hidden.reshape(slot_count, local_count, local_width)
    slots = slot_positions(expert_ids)
    local = 0
    partials = [jnp.dot(hidden[:, local, :], merged[local], preferred_element_type=jnp.float32)]
    tables = [combine_table(expert_ids, slots, combine_weights, first + local, slot_count)]
    share = tok_group // lax.axis_size("tensor")
    local = 0
    rows = tables[local]
    total = jnp.dot(rows, partials[local], precision=lax.Precision.HIGHEST)
    whole = lax.psum(total, "tensor")
    mine_rows = lax.dynamic_slice_in_dim(whole, lax.axis_index("tensor") * share, share, 0)
    return (stepped_factor_a, stepped_factor_b, mine_rows.astype(jnp.bfloat16))


def solution(mesh):
    placed = (
        P("dp", None, "tensor"),
        P("dp", "tensor", None),
        P("dp", "tensor"),
        P("dp", "tensor"),
        P(("tensor", "dp"), None),
        P(("tensor", "dp"), None),
        P("tensor", None),
        P("dp", "tensor"),
        P("dp", None),
        P("dp", None),
    )
    return jax.shard_map(
        body,
        mesh=mesh,
        in_specs=placed,
        out_specs=(P("dp", "tensor"), P(("tensor", "dp"), None), P(("dp", "tensor"), None)),
        check_vma=False,
    )
```

profile of v0, /device:TPU:1, one launch (start us, length us, event | category | flops | bytes accessed | tf_op | source)
XLA Modules:
  0.0 439.5 jit_solution(3945679547135064627)
XLA Ops:
  7.2 0.0 copy-start
  7.2 0.0 copy-start.2
  7.2 0.0 copy-start.1
  7.2 0.0 reduce-scatter.5.cloned.1.call-start
  7.2 0.7 reduce-scatter.5.cloned.1.call-update
  7.9 0.0 reduce-scatter.7.cloned.1.call-start
  8.0 1.6 copy.26
  9.6 0.0 reduce-scatter.7.cloned.1.call-update
  9.6 0.0 all-gather.2.cloned.1.call-start
  9.7 96.7 %reduce-scatter.5.cloned.1.call-done = f32[32,128]{1,0:T(8,128)} async-done(((f32[512,128]{1,0:T(8,128)}), f32[32,128]{1,0:T(8,128)}) %reduce-scatter.5.cloned.1.call-update) | async-done | bytes 16400 | tf_op jit(solution)/shard_map/reduce_scatter | solution.py:45
  106.4 1.4 fusion.10
  107.8 40.5 %all_gather.10 = bf16[32,4096]{1,0:T(8,128)(2,1)} all-gather(bf16[32,128]{1,0:T(8,128)(2,1)S(1)} %get-tuple-element.3), channel_id=1, replica_groups=mesh['dp'=16,'tensor'=32] {'tensor'}, dimensions={1}, use_global_device_ids=true | all-gather | bytes 270336 | tf_op jit(solution)/shard_map/all_gather | solution.py:50
  148.2 0.0 all-gather.2.cloned.1.call-update
  148.3 0.8 copy.27
  149.1 0.1 eq.52
  149.2 0.1 eq.48
  149.4 4.5 %reduce-window.6 = s32[16,16,128]{2,1,0:T(8,128)S(1)} reduce-window(s32[16,16,128]{2,1,0:T(8,128)S(1)} %fusion.7, s32[]{:T(128)} %constant.10.clone.1), window={size=1x1x128 pad=0_0x0_0x127_0}, to_apply=%region_2.3 | reduce-window | flops 4161536 | bytes 262148 | tf_op jit(solution)/shard_map/reduce-window
  153.9 0.4 slice_reduce_fusion
  154.3 0.2 reduce-window.9
  154.5 0.1 broadcast_add_fusion
  154.6 0.1 fusion.6
  154.7 0.1 eq.56
  154.8 0.1 copy.29
  154.9 0.7 broadcast_compare_fusion
  155.6 1.1 select_reduce_fusion
  156.6 42.4 %reduce-scatter.7.cloned.1.call-done = f32[24,32]{1,0:T(8,128)} async-done(((f32[384,32]{1,0:T(8,128)}), f32[24,32]{1,0:T(8,128)}) %reduce-scatter.7.cloned.1.call-update) | async-done | bytes 3088
  199.0 0.0 copy-done.2
  199.0 0.0 copy-done.1
  199.0 1.3 fusion.11
  200.4 38.2 %all_gather.9 = bf16[384,32]{1,0:T(8,128)(2,1)} all-gather(bf16[24,32]{1,0:T(8,128)(2,1)S(1)} %get-tuple-element.5), channel_id=1, replica_groups=mesh['dp'=16,'tensor'=32] {'dp'}, dimensions={0}, use_global_device_ids=true | all-gather | bytes 26112 | tf_op jit(solution)/shard_map/all_gather | solution.py:56
  238.5 42.8 %all-gather.2.cloned.1.call-done = bf16[512,4096]{1,0:T(8,128)(2,1)} async-done(((bf16[32,4096]{1,0:T(8,128)(2,1)}), bf16[512,4096]{1,0:T(8,128)(2,1)}) %all-gather.2.cloned.1.call-update) | async-done | bytes 4194320 | tf_op jit(solution)/shard_map/all_gather | solution.py:54
  281.3 0.0 copy-done
  281.3 3.8 fusion
  285.1 5.2 %fusion.12 = f32[256,4096]{1,0:T(8,128)} fusion(f32[256,192]{0,1:T(8,128)S(1)} %select_reduce_fusion, f32[4096,192]{0,1:T(8,128)S(1)} %fusion), kind=kOutput, calls=%fused_computation.22 | convolution fusion | flops 2415919104 | bytes 7536640 | tf_op jit(solution)/shard_map/dot_general | solution.py:71
  290.3 142.0 %all-reduce.2 = bf16[256,4096]{1,0:T(8,128)(2,1)S(1)} all-reduce(f32[256,4096]{1,0:T(8,128)} %fusion.12), channel_id=1, replica_groups=mesh['dp'=16,'tensor'=32] {'tensor'}, use_global_device_ids=true, to_apply=%region_6.7 | all-reduce | flops 1048576 | bytes 6291456 | tf_op jit(solution)/shard_map/psum | solution.py:72
  432.3 0.6 dynamic-slice_convert_fusion
  (1 shorter events, 0.0 us)
Async XLA Ops:
  7.2 274.2 %copy-start = (bf16[192,384]{1,0:T(8,128)(2,1)S(1)}, bf16[192,384]{1,0:T(8,128)(2,1)}, u32[]{:S(2)}) copy-start(bf16[192,384]{1,0:T(8,128)(2,1)} %param.17) | copy-start | bytes 442372
  7.2 191.9 %copy-start.2 = (f32[24,32]{1,0:T(8,128)S(1)}, f32[24,32]{1,0:T(8,128)}, u32[]{:S(2)}) copy-start(f32[24,32]{1,0:T(8,128)} %param.15) | copy-start | bytes 9220
  7.2 191.9 %copy-start.1 = (f32[24,32]{1,0:T(8,128)S(1)}, f32[24,32]{1,0:T(8,128)}, u32[]{:S(2)}) copy-start(f32[24,32]{1,0:T(8,128)} %param.14) | copy-start | bytes 9220
  7.2 99.2 %reduce-scatter.5.cloned.1.call-start = ((), (), s32[]{:S(2)}) async-start(), calls=%async_computation.2 | async-start | bytes 278528 | tf_op jit(solution)/shard_map/reduce_scatter | solution.py:45
  7.9 191.1 %reduce-scatter.7.cloned.1.call-start = ((), (), s32[]{:S(2)}) async-start(), calls=%async_computation.4 | async-start | bytes 208896
  9.6 271.7 %all-gather.2.cloned.1.call-start = ((), (), s32[]{:S(2)}) async-start(), calls=%async_computation.3 | async-start | bytes 4456448 | tf_op jit(solution)/shard_map/all_gather | solution.py:54
Sparse Core Ops, SparseCore 0:
  12.1 94.2 reduce-scatter.4
  111.0 88.0 reduce-scatter.6
  202.1 79.2 all-gather.1
where the time goes:
time: 442 us; the launch traced here: 440 us
  blocking collectives  221 us (50%)
  waiting for transfers between devices  183 us (41%)
  between operations  13.9 us (3%)
  other arithmetic  9.34 us (2%)
  matrix products  8.98 us (2%)
    psum x1, blocking collectives, body(): whole = lax.psum(total, 'tensor')  142 us
    reduce_scatter x1, waiting for transfers between devices, body(): lax.psum_scatter(grad_a_parts[0], 'dp', scatter_dimension=0, tiled=True)  96.7 us
    unnamed x4, waiting for transfers between devices  43.1 us
    all_gather x1, waiting for transfers between devices, body(): every = lax.all_gather(wide_a, 'dp', axis=0, tiled=True)  42.8 us
    all_gather x1, blocking collectives, body(): lax.all_gather(stepped_factor_a.astype(jnp.bfloat16), 'tensor', axis=1, t...  40.5 us
    all_gather x1, blocking collectives, body(): lax.all_gather(stepped_factor_b.astype(jnp.bfloat16), 'dp', axis=0, tiled...  38.2 us
  transfers between devices with their start and end apart: 3, of which 3 were waited for; matrix products, arithmetic and copies ran while one was open for 3% of the time, Pallas kernels for 0%

commit v1 on v0

v1 whole, which is shorter than its diff:
```python
import jax
import jax.numpy as jnp
from jax import lax
from jax.experimental import pallas as pl
from jax.experimental.pallas import tpu as pltpu
from jax.sharding import PartitionSpec as P

MOMENTUM = 0.9
RATE = 0.5
RANK = 32
B_ROWS = 24
CHUNK = 48
OWNERS = 16
CHIPS = 16
SLOTS = 192
TOKENS = 256
HALF = 128
WIDTH = 4096
TILE = 1024
F32 = jnp.float32
BF16 = jnp.bfloat16


def pack_b(block):
    tail = jnp.concatenate([block[16:24], jnp.zeros((8, RANK), F32)], axis=0)
    return jnp.concatenate([block[0:16], tail, jnp.zeros((16, 64), F32)], axis=1)


def pack_kernel(grad_a, grad_b, out):
    for owner in range(OWNERS):
        out[owner, 0:RANK, :] = grad_a[0, owner * RANK : (owner + 1) * RANK, :].astype(BF16)
        block = grad_b[0, owner * B_ROWS : (owner + 1) * B_ROWS, :]
        out[owner, RANK:CHUNK, :] = pack_b(block).astype(BF16)


def step_kernel(parts, factor_a, moment_a, factor_b, moment_b, new_a, new_b, send_a, send_b):
    total = parts[0].astype(F32)
    for owner in range(1, OWNERS):
        total = total + parts[owner].astype(F32)
    stepped_a = factor_a[...] - RATE * (MOMENTUM * moment_a[...] + total[0:RANK])
    grad_b = jnp.concatenate([total[RANK:CHUNK, 0:32], total[RANK : RANK + 8, 32:64]], axis=0)
    stepped_b = factor_b[...] - RATE * (MOMENTUM * moment_b[...] + grad_b)
    new_a[...] = stepped_a
    new_b[...] = stepped_b
    send_a[...] = stepped_a.astype(BF16)
    send_b[...] = pack_b(stepped_b).astype(BF16)


def base_kernel(ids, weights, hidden, base, send, own, rows, row_weights, slot_scr, weight_scr, order_scr):
    index = lax.axis_index("tensor")
    expert, core = index // 2, index % 2

    @pl.when(pl.program_id(0) == 0)
    def _():
        named = ids[...] == expert
        hit = jnp.sum(jnp.where(named, 1.0, 0.0), axis=1, keepdims=True)
        weight = jnp.sum(jnp.where(named, weights[...], 0.0), axis=1, keepdims=True)
        hit = jnp.broadcast_to(hit, (TOKENS, 128))
        row = lax.broadcasted_iota(jnp.int32, (TOKENS, TOKENS), 0)
        column = lax.broadcasted_iota(jnp.int32, (TOKENS, TOKENS), 1)
        earlier = jnp.where(column < row, 1.0, 0.0).astype(BF16)
        before = jnp.dot(earlier, hit.astype(BF16), preferred_element_type=F32)
        slot_scr[...] = jnp.where(hit > 0.5, before, -1.0)
        weight_scr[...] = jnp.broadcast_to(weight, (TOKENS, 128))
        for half in range(2):
            side = 1 - core if half == 0 else core
            for chip in range(CHIPS):
                source = pl.ds(pl.multiple_of(chip * 16 + side * 8, 8), 8)
                target = pl.ds(half * HALF + chip * 8, 8)
                order_scr[target, :] = slot_scr[source, :]
                row_weights[target, :] = weight_scr[source, :]
        slots = lax.broadcasted_iota(jnp.int32, (TOKENS, SLOTS), 1)
        chosen = order_scr[:, 0:1].astype(jnp.int32) == slots
        chosen = jnp.where(chosen, 1.0, 0.0).astype(BF16)
        rows[...] = jnp.dot(chosen, hidden[...], preferred_element_type=F32).astype(BF16)

    part = jnp.dot(rows[...], base[...], preferred_element_type=F32) * row_weights[:, 0:1]
    send[...] = part[0:HALF].astype(BF16)
    own[...] = part[HALF:TOKENS].astype(BF16)


def low_rank_kernel(gathered, rows, row_weights, packet, own, b_scr):
    for owner in range(OWNERS):
        packet[owner * RANK : (owner + 1) * RANK, :] = gathered[owner, 0:RANK, :]
        block = gathered[owner, RANK:CHUNK, :].astype(F32)
        b_scr[owner * B_ROWS : owner * B_ROWS + 16, :] = block[:, 0:32]
        b_scr[owner * B_ROWS + 16 : (owner + 1) * B_ROWS, :] = block[0:8, 32:64]
    low = jnp.dot(rows[...], b_scr[...].astype(BF16), preferred_element_type=F32)
    low = low * row_weights[:, 0:1]
    pieces = [low[at : at + 32] for at in range(0, HALF, 32)]
    packet[OWNERS * RANK :, :] = jnp.concatenate(pieces, axis=1).astype(BF16)
    own[...] = low[HALF:TOKENS]


def join_kernel(packets, low, own, other, out):
    core = lax.axis_index("tensor") % 2
    received = packets[1 - core, OWNERS * RANK :, :].astype(F32)
    received = jnp.concatenate([received[:, at : at + 32] for at in range(0, 128, 32)], axis=0)
    low = (low[...] + received).astype(BF16)
    step = pl.program_id(0)
    blocks = TILE // 256
    for block in range(blocks):
        at = pl.ds(pl.multiple_of((step * blocks + block) * RANK, RANK), RANK)
        factor = jnp.concatenate([packets[0, at, :], packets[1, at, :]], axis=1)
        columns = slice(block * 256, (block + 1) * 256)
        update = jnp.dot(low, factor, preferred_element_type=F32)
        total = own[:, columns].astype(F32) + other[:, columns].astype(F32) + update
        out[:, columns] = total.astype(BF16)


def shape(dims, dtype):
    return jax.ShapeDtypeStruct(dims, dtype)


def whole(dims):
    return pl.BlockSpec(dims, lambda step: (0,) * len(dims))


def body(
    grad_a_parts,
    grad_b_parts,
    factor_a,
    moment_a,
    factor_b,
    moment_b,
    base_down,
    slot_hidden,
    expert_ids,
    combine_weights,
):
    n_dp = lax.axis_size("dp")
    n_tensor = lax.axis_size("tensor")
    n_chips = n_tensor // 2
    same_core = [[chip * 2 + core for chip in range(n_chips)] for core in range(2)]
    pairs = [[chip * 2, chip * 2 + 1] for chip in range(n_chips)]
    swap = [(index, index ^ 1) for index in range(n_tensor)]
    cross = [
        ((a * n_chips + b) * 2 + core, (b * n_chips + a) * 2 + core)
        for a in range(n_dp)
        for b in range(n_chips)
        for core in range(2)
    ]
    packed = pl.pallas_call(
        pack_kernel,
        out_shape=shape((OWNERS, CHUNK, 128), BF16),
    )(grad_a_parts, grad_b_parts)
    parts = lax.all_to_all(packed, "dp", 0, 0, tiled=True)
    new_a, new_b, send_a, send_b = pl.pallas_call(
        step_kernel,
        out_shape=(
            shape((RANK, 128), F32),
            shape((B_ROWS, RANK), F32),
            shape((RANK, 128), BF16),
            shape((16, 128), BF16),
        ),
    )(parts, factor_a, moment_a, factor_b, moment_b)
    crossed = lax.ppermute(send_a, ("dp", "tensor"), cross)
    steps = WIDTH // TILE
    tile = pl.BlockSpec((HALF, TILE), lambda step: (0, step))
    send, own, rows, row_weights = pl.pallas_call(
        base_kernel,
        grid=(steps,),
        in_specs=[
            whole((TOKENS, 8)),
            whole((TOKENS, 8)),
            whole((SLOTS, 384)),
            pl.BlockSpec((384, TILE), lambda step: (0, step)),
        ],
        out_specs=[tile, tile, whole((TOKENS, 384)), whole((TOKENS, 128))],
        out_shape=(
            shape((HALF, WIDTH), BF16),
            shape((HALF, WIDTH), BF16),
            shape((TOKENS, 384), BF16),
            shape((TOKENS, 128), F32),
        ),
        scratch_shapes=[pltpu.VMEM((TOKENS, 128), F32) for _ in range(3)],
        cost_estimate=pl.CostEstimate(
            flops=2 * TOKENS * 384 * WIDTH, bytes_accessed=6 * 1024 * 1024, transcendentals=0
        ),
    )(expert_ids, combine_weights, slot_hidden, base_down)
    other = lax.ppermute(send, "tensor", swap)
    chunk = jnp.concatenate([crossed, send_b], axis=0)
    spread = jnp.broadcast_to(chunk[None], (n_dp, CHUNK, 128))
    gathered = lax.all_to_all(spread, "dp", 0, 0, tiled=True)
    packet, low = pl.pallas_call(
        low_rank_kernel,
        out_shape=(shape((OWNERS * RANK + 32, 128), BF16), shape((HALF, RANK), F32)),
        scratch_shapes=[pltpu.VMEM((OWNERS * B_ROWS, RANK), F32)],
    )(gathered, rows, row_weights)
    packets = lax.all_gather(packet, "tensor", axis_index_groups=pairs)
    joined = pl.pallas_call(
        join_kernel,
        grid=(steps,),
        in_specs=[whole((2, OWNERS * RANK + 32, 128)), whole((HALF, RANK)), tile, tile],
        out_specs=tile,
        out_shape=shape((HALF, WIDTH), BF16),
    )(packets, low, own, other)
    partials = lax.all_to_all(
        joined.reshape(CHIPS, 8, WIDTH), "tensor", 0, 0, tiled=True, axis_index_groups=same_core
    )
    scored = jnp.sum(partials.astype(F32), axis=0).astype(BF16)
    return new_a, new_b, scored


def solution(mesh):
    placed = (
        P("dp", None, "tensor"),
        P("dp", "tensor", None),
        P("dp", "tensor"),
        P("dp", "tensor"),
        P(("tensor", "dp"), None),
        P(("tensor", "dp"), None),
        P("tensor", None),
        P("dp", "tensor"),
        P("dp", None),
        P("dp", None),
    )
    return jax.shard_map(
        body,
        mesh=mesh,
        in_specs=placed,
        out_specs=(P("dp", "tensor"), P(("tensor", "dp"), None), P(("dp", "tensor"), None)),
        check_vma=False,
    )
```

time: 442 us -> 120 us (0.27)
  waiting for transfers between devices: 183 us -> 0.01 us
  blocking collectives: 221 us -> 85.5 us
  Pallas kernels: 0 us -> 15.1 us
  between operations: 13.9 us -> 0.67 us
  starting transfers between devices: 0.12 us -> 10.1 us
  matrix products: 8.98 us -> 0 us
  other arithmetic: 9.34 us -> 1.45 us
    psum x1 -> x0, blocking collectives: 142 us -> none  [body(): whole = lax.psum(total, 'tensor')]
    reduce_scatter x1 -> x0, waiting for transfers between devices: 96.7 us -> none  [body(): lax.psum_scatter(grad_a_parts[0], 'dp', scatter_dimension=0, tiled=True)]
    all_to_all x0 -> x3, blocking collectives: none -> 78 us  [the longest x1 34.4 us: body(): lax.all_to_all(joined.reshape(CHIPS, 8, WIDTH), 'tensor', 0, 0, tiled=Tru...]
    all_gather x2 -> x1, blocking collectives: 78.6 us -> 7.48 us  [body(): packets = lax.all_gather(packet, 'tensor', axis_index_groups=pairs)]
    unnamed x4 -> x0, waiting for transfers between devices: 43.1 us -> none
    all_gather x1 -> x0, waiting for transfers between devices: 42.8 us -> none  [body(): every = lax.all_gather(wide_a, 'dp', axis=0, tiled=True)]
    pallas_call x0 -> x5, Pallas kernels: none -> 15.1 us  [the longest x1 5.37 us: body(): pl.pallas_call(base_kernel, grid=(steps,), in_specs=[whole((TOKENS, 8)),...]
    ppermute x0 -> x2, starting transfers between devices: none -> 10.1 us  [the longest x1 8.78 us: body(): other = lax.ppermute(send, 'tensor', swap)]
  transfers between devices with their start and end apart: 3 -> 2, of which waited for: 3 -> 0; matrix products, arithmetic and copies ran while one was open for 3% -> 1% of each run, Pallas kernels for 0% -> 5%
where the time goes in v1:
time: 120 us; the launch traced here: 118 us
  blocking collectives  85.5 us (71%)
  Pallas kernels  15.1 us (13%)
  starting transfers between devices  10.1 us (8%)
  local copies, waits for them, and re-layouts  4.83 us (4%)
  other arithmetic  1.45 us (1%)
    all_to_all x1, blocking collectives, body(): lax.all_to_all(joined.reshape(CHIPS, 8, WIDTH), 'tensor', 0, 0, tiled=Tru...  34.4 us
    all_to_all x1, blocking collectives, body(): gathered = lax.all_to_all(spread, 'dp', 0, 0, tiled=True)  29.2 us
    all_to_all x1, blocking collectives, body(): parts = lax.all_to_all(packed, 'dp', 0, 0, tiled=True)  14.5 us
    ppermute x1, starting transfers between devices, body(): other = lax.ppermute(send, 'tensor', swap)  8.78 us
    all_gather x1, blocking collectives, body(): packets = lax.all_gather(packet, 'tensor', axis_index_groups=pairs)  7.48 us
    pallas_call x1, Pallas kernels, body(): pl.pallas_call(base_kernel, grid=(steps,), in_specs=[whole((TOKENS, 8)),...  5.37 us
    unnamed x7, local copies, waits for them, and re-layouts  4.8 us
    pallas_call x1, Pallas kernels, body(): pl.pallas_call(join_kernel, grid=(steps,), in_specs=[whole((2, OWNERS * R...  4.18 us
  transfers between devices with their start and end apart: 2, of which 0 were waited for; matrix products, arithmetic and copies ran while one was open for 1% of the time, Pallas kernels for 5%

profile of v1, /device:TPU:1, one launch (start us, length us, event | category | flops | bytes accessed | tf_op | source)
XLA Modules:
  0.0 117.7 jit_solution(8208146597366434785)
XLA Ops:
  0.6 0.0 copy-start.1
  0.6 1.5 %copy.14.ids = s32[256,8]{1,0:T(8,128)} copy(s32[256,8]{0,1:T(8,128)} %param.18) | data formatting | bytes 16384 | tf_op args[8]
  2.1 1.5 %copy.15.weights = f32[256,8]{1,0:T(8,128)} copy(f32[256,8]{0,1:T(8,128)} %param.19) | data formatting | bytes 16384 | tf_op args[9]
  3.6 5.4 %shard_map.123 = (bf16[128,4096]{1,0:T(8,128)(2,1)}, bf16[128,4096]{1,0:T(8,128)(2,1)}, bf16[256,384]{1,0:T(8,128)(2,1)}, f32[256,128]{1,0:T(8,128)}) custom-call(s32[256,8]{1,0:T(8,128)} %copy.14.ids, f32[256,8]{1,0:T(8,128)} %copy.15.weights, bf16[192,384]{1,0:T(8,128)(2,1)} %hidden.1, bf16[384,4096]{1,0:T(8,128)(2,1)} %base.1), custom_call_target="tpu_custom_call" | custom-call | flops 805306368 | bytes 6291456 | tf_op jit(solution)/shard_map/pallas_call | solution.py:160
  9.0 8.8 %collective-permute-start.1 = (bf16[128,4096]{1,0:T(8,128)(2,1)}, bf16[128,4096]{1,0:T(8,128)(2,1)S(1)}, u32[]{:S(2)}, u32[]{:S(2)}) collective-permute-start(bf16[128,4096]{1,0:T(8,128)(2,1)} %get-tuple-element.22), channel_id=1, source_target_pairs={{0,1},{1,0},{2,3},{3,2},{4,5},{5,4},{6,7},{7,6},{8,9},{9,8},{10,11... | collective-permute-start | bytes 3145736 | tf_op jit(solution)/shard_map/ppermute | solution.py:181
  17.8 0.0 copy-done.1
  17.8 0.8 copy.13.grad_b
  18.6 1.8 %shard_map.121 = bf16[16,48,128]{2,1,0:T(8,128)(2,1)} custom-call(f32[1,512,128]{2,1,0:T(8,128)} %grad_a.1, f32[1,384,32]{2,1,0:T(8,128)} %copy.13.grad_b), custom_call_target="tpu_custom_call" | custom-call | tf_op jit(solution)/shard_map/pallas_call | solution.py:143
  20.3 14.5 %all_to_all.15.parts = bf16[16,48,128]{2,1,0:T(8,128)(2,1)} all-to-all(bf16[16,48,128]{2,1,0:T(8,128)(2,1)} %shard_map.121), channel_id=1, replica_groups=mesh['dp'=16,'tensor'=32] {'dp'}, dimensions={0} | all-to-all | bytes 393216 | tf_op jit(solution)/shard_map/all_to_all | solution.py:147
  34.8 1.7 %shard_map.122 = (f32[32,128]{1,0:T(8,128)}, f32[24,32]{1,0:T(8,128)}, bf16[32,128]{1,0:T(8,128)(2,1)}, bf16[16,128]{1,0:T(8,128)(2,1)}) custom-call(bf16[16,48,128]{2,1,0:T(8,128)(2,1)} %all_to_all.15.parts, f32[32,128]{1,0:T(8,128)} %factor_a.1, f32[32,128]{1,0:T(8,128)} %moment_a.1, f32[24,32]{1,0:T(8,128)} %factor_b.1, f32[24,32]{1,0:T(8,128)} %moment_b.1), custom_call_target="tpu_custom_call" | custom-call | tf_op jit(solution)/shard_map/pallas_call | solution.py:148
  36.5 1.3 %collective-permute-start = (bf16[32,128]{1,0:T(8,128)(2,1)}, bf16[32,128]{1,0:T(8,128)(2,1)S(1)}, u32[]{:S(2)}, u32[]{:S(2)}) collective-permute-start(bf16[32,128]{1,0:T(8,128)(2,1)} %get-tuple-element.15), channel_id=1, source_target_pairs={{0,0},{1,1},{2,32},{3,33},{4,64},{5,65},{6,96},{7,97},{8,128},{9,1... | collective-permute-start | bytes 24584 | tf_op jit(solution)/shard_map/ppermute | solution.py:157
  37.9 0.0 collective-permute-done
  37.9 0.7 pad_maximum_fusion
  38.6 29.2 %all_to_all.16.gathered = bf16[16,48,128]{2,1,0:T(8,128)(2,1)} all-to-all(bf16[16,48,128]{2,1,0:T(8,128)(2,1)S(1)} %broadcast_in_dim.2), channel_id=1, replica_groups=mesh['dp'=16,'tensor'=32] {'dp'}, dimensions={0} | all-to-all | bytes 393216 | tf_op jit(solution)/shard_map/all_to_all | solution.py:184
  67.8 2.1 %shard_map.124 = (bf16[544,128]{1,0:T(8,128)(2,1)}, f32[128,32]{1,0:T(8,128)}) custom-call(bf16[16,48,128]{2,1,0:T(8,128)(2,1)} %all_to_all.16.gathered, bf16[256,384]{1,0:T(8,128)(2,1)} %get-tuple-element.17.rows, f32[256,128]{1,0:T(8,128)} %get-tuple-element.18.row_weights), custom_call_target="tpu_custom_call" | custom-call | tf_op jit(solution)/shard_map/pallas_call | solution.py:185
  69.9 7.5 %all-gather = bf16[1088,128]{1,0:T(8,128)(2,1)} all-gather(bf16[544,128]{1,0:T(8,128)(2,1)} %get-tuple-element.19), channel_id=2, replica_groups={{0,1},{2,3},{4,5},{6,7},{8,9},{10,11},{12,13},{14,15},{16,17},{18,19},{..., dimensions={0}, use_global_device_ids=true | all-gather | bytes 417792 | tf_op jit(solution)/shard_map/all_gather | solution.py:190
  77.4 0.0 collective-permute-done.1.other
  77.4 0.0 copy-start
  77.4 1.0 copy-done
  78.4 4.2 %shard_map.125 = bf16[128,4096]{1,0:T(8,128)(2,1)} custom-call(bf16[2,544,128]{2,1,0:T(8,128)(2,1)} %bitcast.3, f32[128,32]{1,0:T(8,128)} %get-tuple-element.20.low, bf16[128,4096]{1,0:T(8,128)(2,1)} %get-tuple-element.21.own, bf16[128,4096]{1,0:T(8,128)(2,1)} %copy-done), custom_call_target="tpu_custom_call" | custom-call | tf_op jit(solution)/shard_map/pallas_call | solution.py:191
  82.6 34.4 %all_to_all.17 = bf16[16,8,4096]{2,1,0:T(8,128)(2,1)S(1)} all-to-all(bf16[16,8,4096]{2,1,0:T(8,128)(2,1)} %bitcast.2), channel_id=1, replica_groups={{0,2,4,6,8,10,12,14,16,18,20,22,24,26,28,30},{1,3,5,7,9,11,13,15,17,19,..., dimensions={0} | all-to-all | bytes 2097152 | tf_op jit(solution)/shard_map/all_to_all | solution.py:198
  116.9 0.8 reduce_sum.12
  (1 shorter events, 0.0 us)
Async XLA Ops:
  0.6 17.2 %copy-start.1 = (f32[1,384,32]{1,2,0:T(8,128)S(1)}, f32[1,384,32]{1,2,0:T(8,128)}, u32[]{:S(2)}) copy-start(f32[1,384,32]{1,2,0:T(8,128)} %param.11) | copy-start | bytes 147460
  9.0 68.4 %collective-permute-start.1 = (bf16[128,4096]{1,0:T(8,128)(2,1)}, bf16[128,4096]{1,0:T(8,128)(2,1)S(1)}, u32[]{:S(2)}, u32[]{:S(2)}) collective-permute-start(bf16[128,4096]{1,0:T(8,128)(2,1)} %get-tuple-element.22), channel_id=1, source_target_pairs={{0,1},{1,0},{2,3},{3,2},{4,5},{5,4},{6,7},{7,6},{8,9},{9,8},{10,11... | collective-permute-start | bytes 3145736 | tf_op jit(solution)/shard_map/ppermute | solution.py:181
  36.5 1.3 %collective-permute-start = (bf16[32,128]{1,0:T(8,128)(2,1)}, bf16[32,128]{1,0:T(8,128)(2,1)S(1)}, u32[]{:S(2)}, u32[]{:S(2)}) collective-permute-start(bf16[32,128]{1,0:T(8,128)(2,1)} %get-tuple-element.15), channel_id=1, source_target_pairs={{0,0},{1,1},{2,32},{3,33},{4,64},{5,65},{6,96},{7,97},{8,128},{9,1... | collective-permute-start | bytes 24584 | tf_op jit(solution)/shard_map/ppermute | solution.py:157
  77.4 1.0 copy-start

commit v2 on v1

v2 whole, which is shorter than its diff:
```python
import jax
import jax.numpy as jnp
from jax import lax
from jax.experimental import pallas as pl
from jax.experimental.pallas import tpu as pltpu
from jax.sharding import PartitionSpec as P

MOMENTUM = 0.9
RATE = 0.5
RANK = 32
B_ROWS = 24
CHUNK = 48
OWNERS = 16
SLOTS = 192
TOKENS = 256
HIDDEN = 384
WIDTH = 4096
QUARTER = 1024
TILE = 1024
RING = 8
F32 = jnp.float32
BF16 = jnp.bfloat16


def pack_b(block):
    tail = jnp.concatenate([block[16:24], jnp.zeros((8, RANK), F32)], axis=0)
    return jnp.concatenate([block[0:16], tail, jnp.zeros((16, 64), F32)], axis=1)


def pack_kernel(grad_a, grad_b, out):
    columns = grad_b[0].T
    for owner in range(OWNERS):
        out[owner, 0:RANK, :] = grad_a[0, owner * RANK : (owner + 1) * RANK, :].astype(BF16)
        block = columns[owner * B_ROWS : (owner + 1) * B_ROWS, :]
        out[owner, RANK:CHUNK, :] = pack_b(block).astype(BF16)


def step_kernel(parts, factor_a, moment_a, factor_b, moment_b, new_a, new_b, spread):
    total = parts[0].astype(F32)
    for owner in range(1, OWNERS):
        total = total + parts[owner].astype(F32)
    stepped_a = factor_a[...] - RATE * (MOMENTUM * moment_a[...] + total[0:RANK])
    grad_b = jnp.concatenate([total[RANK:CHUNK, 0:32], total[RANK : RANK + 8, 32:64]], axis=0)
    stepped_b = factor_b[...] - RATE * (MOMENTUM * moment_b[...] + grad_b)
    new_a[...] = stepped_a
    new_b[...] = stepped_b
    chunk = jnp.concatenate([stepped_a, pack_b(stepped_b)], axis=0).astype(BF16)
    for owner in range(OWNERS):
        spread[owner] = chunk


def base_kernel(after, ids, weights, hidden, base, send, own, rows, row_weights):
    index = lax.axis_index("tensor")
    expert, core = index // 2, index % 2

    @pl.when(pl.program_id(0) == 0)
    def _():
        named = ids[...] == expert
        hit = jnp.sum(jnp.where(named, 1.0, 0.0), axis=0, keepdims=True)
        weight = jnp.sum(jnp.where(named, weights[...], 0.0), axis=0, keepdims=True)
        row = lax.broadcasted_iota(jnp.int32, (TOKENS, TOKENS), 0)
        column = lax.broadcasted_iota(jnp.int32, (TOKENS, TOKENS), 1)
        earlier = jnp.where(row < column, 1.0, 0.0).astype(BF16)
        wide = jnp.broadcast_to(hit, (8, TOKENS)).astype(BF16)
        before = jnp.dot(wide, earlier, preferred_element_type=F32)[0:1]
        slot = jnp.where(hit > 0.5, before, -1.0)
        both = jnp.concatenate([slot, weight, jnp.zeros((6, TOKENS), F32)], axis=0).T
        slots = lax.broadcasted_iota(jnp.int32, (TOKENS, SLOTS), 1)
        chosen = jnp.where(both[:, 0:1].astype(jnp.int32) == slots, 1.0, 0.0).astype(BF16)
        rows[...] = jnp.dot(chosen, hidden[...], preferred_element_type=F32).astype(BF16)
        row_weights[...] = jnp.broadcast_to(both[:, 1:2], (TOKENS, 128))

    part = jnp.dot(rows[...], base[...], preferred_element_type=F32) * row_weights[:, 0:1]
    for mine in range(2):

        @pl.when(core == mine)
        def _(mine=mine):
            for block in range(TILE // 128):
                ring, low, side = block // 4, block // 2 % 2, block % 2
                piece = part[:, block * 128 : (block + 1) * 128]
                columns = slice(ring * 128, (ring + 1) * 128)
                if side == mine:
                    own[low, :, columns] = piece
                else:
                    send[low, :, columns] = piece.astype(BF16)


def middle_kernel(own, other, send, keep):
    low = lax.axis_index("tensor") // 2 % 2
    send[...] = (own[1 - low] + other[1 - low].astype(F32)).astype(BF16)
    keep[...] = own[low] + other[low].astype(F32)


def low_rank_kernel(gathered, rows, row_weights, packet, b_scr):
    for owner in range(OWNERS):
        block = gathered[owner, RANK:CHUNK, :].astype(F32)
        b_scr[owner * B_ROWS : owner * B_ROWS + 16, :] = block[:, 0:32]
        b_scr[owner * B_ROWS + 16 : (owner + 1) * B_ROWS, :] = block[0:8, 32:64]
    low = jnp.dot(rows[...], b_scr[...].astype(BF16), preferred_element_type=F32)
    low = low * row_weights[:, 0:1]
    packet[...] = jnp.concatenate([low[at : at + 64] for at in range(0, TOKENS, 64)], axis=1).astype(BF16)


def join_kernel(packets, factors, keep, other, out):
    sides = []
    for low in range(2):
        total = packets[2 * low].astype(F32) + packets[2 * low + 1].astype(F32)
        sides.append(jnp.concatenate([total[:, at : at + 32] for at in range(0, 128, 32)], axis=0))
    low = jnp.concatenate(sides, axis=1).astype(BF16)
    for pair in range(RING // 2):
        halves = []
        for ring in (2 * pair, 2 * pair + 1):
            halves.append(
                jnp.concatenate([factors[ring, 0:RANK, :], factors[ring, CHUNK : CHUNK + RANK, :]], axis=0)
            )
        factor = jnp.concatenate(halves, axis=1)
        columns = slice(pair * 256, (pair + 1) * 256)
        update = jnp.dot(low, factor, preferred_element_type=F32)
        out[:, columns] = (keep[:, columns] + other[:, columns].astype(F32) + update).astype(BF16)


def add_kernel(parts, out):
    for part in range(4):
        total = parts[part].astype(F32)
        for ring in range(1, RING):
            total = total + parts[ring * 4 + part].astype(F32)
        for ring in range(RING):
            block = ring * 4 + part
            out[:, block * 128 : (block + 1) * 128] = total[:, ring * 128 : (ring + 1) * 128].astype(BF16)


def shape(dims, dtype):
    return jax.ShapeDtypeStruct(dims, dtype)


def whole(dims):
    return pl.BlockSpec(dims, lambda step: (0,) * len(dims))


def body(
    grad_a_parts,
    grad_b_parts,
    factor_a,
    moment_a,
    factor_b,
    moment_b,
    base_down,
    slot_hidden,
    expert_ids,
    combine_weights,
):
    n_tensor = lax.axis_size("tensor")
    quads = [[4 * ring + part for part in range(4)] for ring in range(n_tensor // 4)]
    rings = [[4 * ring + part for ring in range(n_tensor // 4)] for part in range(4)]
    packed = pl.pallas_call(
        pack_kernel,
        out_shape=shape((OWNERS, CHUNK, 128), BF16),
    )(grad_a_parts, jnp.swapaxes(grad_b_parts, 1, 2))
    parts = lax.all_to_all(packed, "dp", 0, 0, tiled=True)
    steps = WIDTH // TILE
    halves = pl.BlockSpec((2, TOKENS, TILE // 4), lambda step: (0, 0, step))
    send, own, rows, row_weights = pl.pallas_call(
        base_kernel,
        grid=(steps,),
        in_specs=[
            pl.BlockSpec(memory_space=pl.ANY),
            whole((8, TOKENS)),
            whole((8, TOKENS)),
            whole((SLOTS, HIDDEN)),
            pl.BlockSpec((HIDDEN, TILE), lambda step: (0, step)),
        ],
        out_specs=[halves, halves, whole((TOKENS, HIDDEN)), whole((TOKENS, 128))],
        out_shape=(
            shape((2, TOKENS, QUARTER), BF16),
            shape((2, TOKENS, QUARTER), F32),
            shape((TOKENS, HIDDEN), BF16),
            shape((TOKENS, 128), F32),
        ),
        cost_estimate=pl.CostEstimate(
            flops=2 * TOKENS * HIDDEN * WIDTH, bytes_accessed=7 * 1024 * 1024, transcendentals=0
        ),
    )(packed, expert_ids.T, combine_weights.T, slot_hidden, base_down)
    other = lax.ppermute(send, "tensor", [(index, index ^ 1) for index in range(n_tensor)])
    new_a, new_b, spread = pl.pallas_call(
        step_kernel,
        out_shape=(
            shape((RANK, 128), F32),
            shape((B_ROWS, RANK), F32),
            shape((OWNERS, CHUNK, 128), BF16),
        ),
    )(parts, factor_a, moment_a, factor_b, moment_b)
    gathered = lax.all_to_all(spread, "dp", 0, 0, tiled=True)
    send_low, keep = pl.pallas_call(
        middle_kernel,
        out_shape=(shape((TOKENS, QUARTER), BF16), shape((TOKENS, QUARTER), F32)),
        cost_estimate=pl.CostEstimate(flops=2**20, bytes_accessed=4 * 2**20, transcendentals=0),
    )(own, other)
    other_low = lax.ppermute(send_low, "tensor", [(index, index ^ 2) for index in range(n_tensor)])
    factors = lax.all_to_all(
        gathered.reshape(RING, 2 * CHUNK, 128), "tensor", 0, 0, tiled=True, axis_index_groups=rings
    )
    packet = pl.pallas_call(
        low_rank_kernel,
        out_shape=shape((64, 128), BF16),
        scratch_shapes=[pltpu.VMEM((OWNERS * B_ROWS, RANK), F32)],
    )(gathered, rows, row_weights)
    packets = lax.all_gather(packet, "tensor", axis_index_groups=quads)
    joined = pl.pallas_call(
        join_kernel,
        out_shape=shape((TOKENS, QUARTER), BF16),
    )(packets, factors, keep, other_low)
    partials = lax.all_to_all(joined.reshape(n_tensor, 8, QUARTER), "tensor", 0, 0, tiled=True)
    scored = pl.pallas_call(
        add_kernel,
        out_shape=shape((8, WIDTH), BF16),
    )(partials)
    return new_a, new_b, scored


def solution(mesh):
    placed = (
        P("dp", None, "tensor"),
        P("dp", "tensor", None),
        P("dp", "tensor"),
        P("dp", "tensor"),
        P(("tensor", "dp"), None),
        P(("tensor", "dp"), None),
        P("tensor", None),
        P("dp", "tensor"),
        P("dp", None),
        P("dp", None),
    )
    return jax.shard_map(
        body,
        mesh=mesh,
        in_specs=placed,
        out_specs=(P("dp", "tensor"), P(("tensor", "dp"), None), P(("dp", "tensor"), None)),
        check_vma=False,
    )
```

time: 120 us -> 99.9 us (0.83); the launches traced: 118 us -> 99.1 us
  blocking collectives: 85.5 us -> 48 us
  starting transfers between devices: 10.1 us -> 25.5 us
  Pallas kernels: 15.1 us -> 19.3 us
  waiting for transfers between devices: 0.01 us -> 3.7 us
  local copies, waits for them, and re-layouts: 4.83 us -> 1.85 us
  other arithmetic: 1.45 us -> 0 us
    all_to_all x2 -> x1, blocking collectives: 63.6 us -> 25 us  [body(): lax.all_to_all(joined.reshape(n_tensor, 8, QUARTER), 'tensor', 0, 0, tile...]
    all_to_all x0 -> x2, starting transfers between devices: none -> 14.8 us  [the longest x1 10.1 us: body(): lax.all_to_all(gathered.reshape(RING, 2 * CHUNK, 128), 'tensor', 0, 0, ti...]
    pallas_call x3 -> x5, Pallas kernels: 11.7 us -> 15.7 us  [the longest x1 6.03 us: body(): pl.pallas_call(base_kernel, grid=(steps,), in_specs=[pl.BlockSpec(memory_...]
    all_to_all x0 -> x2, waiting for transfers between devices: none -> 3.7 us  [the longest x1 3.69 us: body(): gathered = lax.all_to_all(spread, 'dp', 0, 0, tiled=True)]
    unnamed x7 -> x8, local copies, waits for them, and re-layouts: 4.8 us -> 1.85 us
    all_gather x1, blocking collectives: 7.48 us -> 8.68 us  [body(): packets = lax.all_gather(packet, 'tensor', axis_index_groups=quads)]
  transfers between devices with their start and end apart: 2 -> 4, of which waited for: 0 -> 1; matrix products, arithmetic and copies ran while one was open for 1% -> 0% of each run, Pallas kernels for 5% -> 7%
where the time goes in v2:
time: 99.9 us; the launch traced here: 99.1 us
  blocking collectives  48 us (48%)
  starting transfers between devices  25.5 us (26%)
  Pallas kernels  19.3 us (19%)
  waiting for transfers between devices  3.7 us (4%)
  local copies, waits for them, and re-layouts  1.85 us (2%)
    all_to_all x1, blocking collectives, body(): lax.all_to_all(joined.reshape(n_tensor, 8, QUARTER), 'tensor', 0, 0, tile...  25 us
    all_to_all x1, blocking collectives, body(): parts = lax.all_to_all(packed, 'dp', 0, 0, tiled=True)  14.3 us
    all_to_all x1, starting transfers between devices, body(): lax.all_to_all(gathered.reshape(RING, 2 * CHUNK, 128), 'tensor', 0, 0, ti...  10.1 us
    ppermute x1, starting transfers between devices, body(): lax.ppermute(send, 'tensor', [(index, index ^ 1) for index in range(n_ten...  8.79 us
    all_gather x1, blocking collectives, body(): packets = lax.all_gather(packet, 'tensor', axis_index_groups=quads)  8.68 us
    pallas_call x1, Pallas kernels, body(): pl.pallas_call(base_kernel, grid=(steps,), in_specs=[pl.BlockSpec(memory_...  6.03 us
    all_to_all x1, starting transfers between devices, body(): gathered = lax.all_to_all(spread, 'dp', 0, 0, tiled=True)  4.79 us
    all_to_all x1, waiting for transfers between devices, body(): gathered = lax.all_to_all(spread, 'dp', 0, 0, tiled=True)  3.69 us
  transfers between devices with their start and end apart: 4, of which 1 were waited for; matrix products, arithmetic and copies ran while one was open for 0% of the time, Pallas kernels for 7%

profile of v2, /device:TPU:1, one launch (start us, length us, event | category | flops | bytes accessed | tf_op | source)
XLA Modules:
  0.0 99.1 jit_solution(18432802964445412051)
XLA Ops:
  0.6 1.8 %shard_map.121.after = bf16[16,48,128]{2,1,0:T(8,128)(2,1)} custom-call(f32[1,512,128]{2,1,0:T(8,128)} %grad_a.1, f32[1,32,384]{2,1,0:T(8,128)} %bitcast.8), custom_call_target="tpu_custom_call" | custom-call | tf_op jit(solution)/shard_map/pallas_call | solution.py:155
  2.4 0.0 copy-start
  2.4 6.0 %shard_map.123 = (bf16[2,256,1024]{2,1,0:T(8,128)(2,1)}, f32[2,256,1024]{2,1,0:T(8,128)}, bf16[256,384]{1,0:T(8,128)(2,1)}, f32[256,128]{1,0:T(8,128)}) custom-call(bf16[16,48,128]{2,1,0:T(8,128)(2,1)} %shard_map.121.after, s32[8,256]{1,0:T(8,128)} %bitcast.9, f32[8,256]{1,0:T(8,128)} %bitcast.10, bf16[192,384]{1,0:T(8,128)(2,1)} %hidden.1, ...), custom_call_target="tpu_custom_call" | custom-call | flops 805306368 | bytes 7340032 | tf_op jit(solution)/shard_map/pallas_call | solution.py:162
  8.5 8.8 %collective-permute-start = (bf16[2,256,1024]{2,1,0:T(8,128)(2,1)}, bf16[2,256,1024]{2,1,0:T(8,128)(2,1)S(1)}, u32[]{:S(2)}, u32[]{:S(2)}) collective-permute-start(bf16[2,256,1024]{2,1,0:T(8,128)(2,1)} %get-tuple-element.18), channel_id=1, source_target_pairs={{0,1},{1,0},{2,3},{3,2},{4,5},{5,4},{6,7},{7,6},{8,9},{9,8},{10,11... | collective-permute-start | bytes 3145736 | tf_op jit(solution)/shard_map/ppermute | solution.py:183
  17.3 0.0 copy-done
  17.3 14.3 %all_to_all.20.parts = bf16[16,48,128]{2,1,0:T(8,128)(2,1)} all-to-all(bf16[16,48,128]{2,1,0:T(8,128)(2,1)S(1)} %copy-done), channel_id=1, replica_groups=mesh['dp'=16,'tensor'=32] {'dp'}, dimensions={0} | all-to-all | bytes 393216 | tf_op jit(solution)/shard_map/all_to_all | solution.py:159
  31.6 1.8 %shard_map.122 = (f32[32,128]{1,0:T(8,128)}, f32[24,32]{1,0:T(8,128)}, bf16[16,48,128]{2,1,0:T(8,128)(2,1)}) custom-call(bf16[16,48,128]{2,1,0:T(8,128)(2,1)} %all_to_all.20.parts, f32[32,128]{1,0:T(8,128)} %factor_a.1, f32[32,128]{1,0:T(8,128)} %moment_a.1, f32[24,32]{1,0:T(8,128)} %factor_b.1, f32[24,32]{1,0:T(8,128)} %moment_b.1), custom_call_target="tpu_custom_call" | custom-call | tf_op jit(solution)/shard_map/pallas_call | solution.py:184
  33.4 4.8 %all-to-all-start.1 = ((bf16[16,48,128]{2,1,0:T(8,128)(2,1)}), bf16[16,48,128]{2,1,0:T(8,128)(2,1)}, u32[]{:S(2)}, u32[]{:S(2)}) async-start(bf16[16,48,128]{2,1,0:T(8,128)(2,1)} %get-tuple-element.14), calls=%async_computation.1 | async-start | bytes 393216 | tf_op jit(solution)/shard_map/all_to_all | solution.py:192
  38.2 0.0 collective-permute-done.other
  38.2 0.0 copy-start.1
  38.2 1.0 copy-done.1
  39.2 3.1 %shard_map.125 = (bf16[256,1024]{1,0:T(8,128)(2,1)}, f32[256,1024]{1,0:T(8,128)}) custom-call(f32[2,256,1024]{2,1,0:T(8,128)} %get-tuple-element.17.own, bf16[2,256,1024]{2,1,0:T(8,128)(2,1)} %copy-done.1), custom_call_target="tpu_custom_call" | custom-call | flops 1048576 | bytes 4194304 | tf_op jit(solution)/shard_map/pallas_call | solution.py:193
  42.3 1.9 %collective-permute-start.1 = (bf16[256,1024]{1,0:T(8,128)(2,1)}, bf16[256,1024]{1,0:T(8,128)(2,1)S(1)}, u32[]{:S(2)}, u32[]{:S(2)}) collective-permute-start(bf16[256,1024]{1,0:T(8,128)(2,1)} %get-tuple-element.20), channel_id=1, source_target_pairs={{0,2},{1,3},{2,0},{3,1},{4,6},{5,7},{6,4},{7,5},{8,10},{9,11},{10,... | collective-permute-start | bytes 1572872 | tf_op jit(solution)/shard_map/ppermute | solution.py:198
  44.3 3.7 %all-to-all-done.1.gathered = bf16[16,48,128]{2,1,0:T(8,128)(2,1)} async-done(((bf16[16,48,128]{2,1,0:T(8,128)(2,1)}), bf16[16,48,128]{2,1,0:T(8,128)(2,1)}, u32[]{:S(2)}, u32[]{:S(2)}) %all-to-all-start.1) | async-done | bytes 196640 | tf_op jit(solution)/shard_map/all_to_all | solution.py:192
  47.9 10.1 %all-to-all-start.2 = ((bf16[8,96,128]{2,1,0:T(8,128)(2,1)}), bf16[8,96,128]{2,1,0:T(8,128)(2,1)S(1)}, u32[]{:S(2)}, u32[]{:S(2)}) async-start(bf16[8,96,128]{2,1,0:T(8,128)(2,1)} %bitcast.4), calls=%async_computation.2 | async-start | bytes 393216 | tf_op jit(solution)/shard_map/all_to_all | solution.py:199
  58.0 2.1 %shard_map.124 = bf16[64,128]{1,0:T(8,128)(2,1)} custom-call(bf16[16,48,128]{2,1,0:T(8,128)(2,1)} %all-to-all-done.1.gathered, bf16[256,384]{1,0:T(8,128)(2,1)} %get-tuple-element.15.rows, f32[256,128]{1,0:T(8,128)} %get-tuple-element.16.row_weights), custom_call_target="tpu_custom_call" | custom-call | tf_op jit(solution)/shard_map/pallas_call | solution.py:202
  60.1 8.7 %all-gather = bf16[256,128]{1,0:T(8,128)(2,1)} all-gather(bf16[64,128]{1,0:T(8,128)(2,1)} %shard_map.124), channel_id=2, replica_groups={{0,1,2,3},{4,5,6,7},{8,9,10,11},{12,13,14,15},{16,17,18,19},{20,21,22,2..., dimensions={0}, use_global_device_ids=true | all-gather | bytes 81920 | tf_op jit(solution)/shard_map/all_gather | solution.py:207
  68.7 0.0 all-to-all-done.2.factors
  68.7 0.0 copy-start.2
  68.7 0.0 collective-permute-done.1.other
  68.8 0.0 copy-start.3
  68.8 0.7 copy-done.2
  69.4 0.2 copy-done.3
  69.6 2.7 %shard_map.126 = bf16[256,1024]{1,0:T(8,128)(2,1)} custom-call(bf16[4,64,128]{2,1,0:T(8,128)(2,1)} %bitcast.7, bf16[8,96,128]{2,1,0:T(8,128)(2,1)} %copy-done.2, f32[256,1024]{1,0:T(8,128)} %get-tuple-element.19.keep, bf16[256,1024]{1,0:T(8,128)(2,1)} %copy-done.3), custom_call_target="tpu_custom_call" | custom-call | tf_op jit(solution)/shard_map/pallas_call | solution.py:208
  72.3 25.0 %all_to_all.21.parts = bf16[32,8,1024]{2,1,0:T(8,128)(2,1)} all-to-all(bf16[32,8,1024]{2,1,0:T(8,128)(2,1)} %bitcast.6), channel_id=1, replica_groups=mesh['dp'=16,'tensor'=32] {'tensor'}, dimensions={0} | all-to-all | bytes 1048576 | tf_op jit(solution)/shard_map/all_to_all | solution.py:212
  97.4 1.7 %shard_map.127 = bf16[8,4096]{1,0:T(8,128)(2,1)} custom-call(bf16[32,8,1024]{2,1,0:T(8,128)(2,1)} %all_to_all.21.parts), custom_call_target="tpu_custom_call" | custom-call | tf_op jit(solution)/shard_map/pallas_call | solution.py:213
Async XLA Ops:
  2.4 14.8 %copy-start = (bf16[16,48,128]{2,1,0:T(8,128)(2,1)S(1)}, bf16[16,48,128]{2,1,0:T(8,128)(2,1)}, u32[]{:S(2)}) copy-start(bf16[16,48,128]{2,1,0:T(8,128)(2,1)} %shard_map.121.after) | copy-start | bytes 589828
  8.5 29.7 %collective-permute-start = (bf16[2,256,1024]{2,1,0:T(8,128)(2,1)}, bf16[2,256,1024]{2,1,0:T(8,128)(2,1)S(1)}, u32[]{:S(2)}, u32[]{:S(2)}) collective-permute-start(bf16[2,256,1024]{2,1,0:T(8,128)(2,1)} %get-tuple-element.18), channel_id=1, source_target_pairs={{0,1},{1,0},{2,3},{3,2},{4,5},{5,4},{6,7},{7,6},{8,9},{9,8},{10,11... | collective-permute-start | bytes 3145736 | tf_op jit(solution)/shard_map/ppermute | solution.py:183
  33.4 14.6 %all-to-all-start.1 = ((bf16[16,48,128]{2,1,0:T(8,128)(2,1)}), bf16[16,48,128]{2,1,0:T(8,128)(2,1)}, u32[]{:S(2)}, u32[]{:S(2)}) async-start(bf16[16,48,128]{2,1,0:T(8,128)(2,1)} %get-tuple-element.14), calls=%async_computation.1 | async-start | bytes 393216 | tf_op jit(solution)/shard_map/all_to_all | solution.py:192
  38.2 1.0 %copy-start.1 = (bf16[2,256,1024]{2,1,0:T(8,128)(2,1)}, bf16[2,256,1024]{2,1,0:T(8,128)(2,1)S(1)}, u32[]{:S(2)}) copy-start(bf16[2,256,1024]{2,1,0:T(8,128)(2,1)S(1)} %collective-permute-done.other) | copy-start | bytes 3145732
  42.3 26.4 %collective-permute-start.1 = (bf16[256,1024]{1,0:T(8,128)(2,1)}, bf16[256,1024]{1,0:T(8,128)(2,1)S(1)}, u32[]{:S(2)}, u32[]{:S(2)}) collective-permute-start(bf16[256,1024]{1,0:T(8,128)(2,1)} %get-tuple-element.20), channel_id=1, source_target_pairs={{0,2},{1,3},{2,0},{3,1},{4,6},{5,7},{6,4},{7,5},{8,10},{9,11},{10,... | collective-permute-start | bytes 1572872 | tf_op jit(solution)/shard_map/ppermute | solution.py:198
  47.9 20.8 %all-to-all-start.2 = ((bf16[8,96,128]{2,1,0:T(8,128)(2,1)}), bf16[8,96,128]{2,1,0:T(8,128)(2,1)S(1)}, u32[]{:S(2)}, u32[]{:S(2)}) async-start(bf16[8,96,128]{2,1,0:T(8,128)(2,1)} %bitcast.4), calls=%async_computation.2 | async-start | bytes 393216 | tf_op jit(solution)/shard_map/all_to_all | solution.py:199
  68.7 0.7 copy-start.2
  68.8 0.9 copy-start.3

commit v3 on v2

--- a/solution.py
+++ b/solution.py
@@ -27,6 +27,10 @@
     return jnp.concatenate([block[0:16], tail, jnp.zeros((16, 64), F32)], axis=1)
 
 
+def first_rows(a, b):
+    return lax.dot_general(a, b, (((0,), (0,)), ((), ())), preferred_element_type=F32)
+
+
 def pack_kernel(grad_a, grad_b, out):
     columns = grad_b[0].T
     for owner in range(OWNERS):
@@ -49,7 +53,7 @@
         spread[owner] = chunk
 
 
-def base_kernel(after, ids, weights, hidden, base, send, own, rows, row_weights):
+def base_kernel(after, ids, weights, hidden, base, send, own, rows_t, row_weights, rows, column):
     index = lax.axis_index("tensor")
     expert, core = index // 2, index % 2
 
@@ -58,9 +62,9 @@
         named = ids[...] == expert
         hit = jnp.sum(jnp.where(named, 1.0, 0.0), axis=0, keepdims=True)
         weight = jnp.sum(jnp.where(named, weights[...], 0.0), axis=0, keepdims=True)
-        row = lax.broadcasted_iota(jnp.int32, (TOKENS, TOKENS), 0)
-        column = lax.broadcasted_iota(jnp.int32, (TOKENS, TOKENS), 1)
-        earlier = jnp.where(row < column, 1.0, 0.0).astype(BF16)
+        one = lax.broadcasted_iota(jnp.int32, (TOKENS, TOKENS), 0)
+        two = lax.broadcasted_iota(jnp.int32, (TOKENS, TOKENS), 1)
+        earlier = jnp.where(one < two, 1.0, 0.0).astype(BF16)
         wide = jnp.broadcast_to(hit, (8, TOKENS)).astype(BF16)
         before = jnp.dot(wide, earlier, preferred_element_type=F32)[0:1]
         slot = jnp.where(hit > 0.5, before, -1.0)
@@ -68,9 +72,13 @@
         slots = lax.broadcasted_iota(jnp.int32, (TOKENS, SLOTS), 1)
         chosen = jnp.where(both[:, 0:1].astype(jnp.int32) == slots, 1.0, 0.0).astype(BF16)
         rows[...] = jnp.dot(chosen, hidden[...], preferred_element_type=F32).astype(BF16)
-        row_weights[...] = jnp.broadcast_to(both[:, 1:2], (TOKENS, 128))
-
-    part = jnp.dot(rows[...], base[...], preferred_element_type=F32) * row_weights[:, 0:1]
+        column[...] = jnp.broadcast_to(both[:, 1:2], (TOKENS, 128))
+        slots_t = lax.broadcasted_iota(jnp.int32, (SLOTS, TOKENS), 0)
+        chosen_t = jnp.where(slot.astype(jnp.int32) == slots_t, 1.0, 0.0).astype(BF16)
+        rows_t[...] = first_rows(hidden[...], chosen_t).astype(BF16)
+        row_weights[...] = jnp.broadcast_to(weight, (8, TOKENS))
+
+    part = jnp.dot(rows[...], base[...], preferred_element_type=F32) * column[:, 0:1]
     for mine in range(2):
 
         @pl.when(core == mine)
@@ -91,31 +99,24 @@
     keep[...] = own[low] + other[low].astype(F32)
 
 
-def low_rank_kernel(gathered, rows, row_weights, packet, b_scr):
+def low_rank_kernel(gathered, rows_t, row_weights, low, b_scr):
     for owner in range(OWNERS):
         block = gathered[owner, RANK:CHUNK, :].astype(F32)
         b_scr[owner * B_ROWS : owner * B_ROWS + 16, :] = block[:, 0:32]
         b_scr[owner * B_ROWS + 16 : (owner + 1) * B_ROWS, :] = block[0:8, 32:64]
-    low = jnp.dot(rows[...], b_scr[...].astype(BF16), preferred_element_type=F32)
-    low = low * row_weights[:, 0:1]
-    packet[...] = jnp.concatenate([low[at : at + 64] for at in range(0, TOKENS, 64)], axis=1).astype(BF16)
-
-
-def join_kernel(packets, factors, keep, other, out):
-    sides = []
-    for low in range(2):
-        total = packets[2 * low].astype(F32) + packets[2 * low + 1].astype(F32)
-        sides.append(jnp.concatenate([total[:, at : at + 32] for at in range(0, 128, 32)], axis=0))
-    low = jnp.concatenate(sides, axis=1).astype(BF16)
+    low[...] = (first_rows(b_scr[...].astype(BF16), rows_t[...]) * row_weights[0:1, :]).astype(BF16)
+
+
+def join_kernel(lows, factors, keep, other, out):
+    sides = [lows[2 * side].astype(F32) + lows[2 * side + 1].astype(F32) for side in range(2)]
+    low = jnp.concatenate(sides, axis=0).astype(BF16)
     for pair in range(RING // 2):
-        halves = []
-        for ring in (2 * pair, 2 * pair + 1):
-            halves.append(
-                jnp.concatenate([factors[ring, 0:RANK, :], factors[ring, CHUNK : CHUNK + RANK, :]], axis=0)
-            )
-        factor = jnp.concatenate(halves, axis=1)
+        halves = [
+            jnp.concatenate([factors[ring, 0:RANK, :], factors[ring, CHUNK : CHUNK + RANK, :]], axis=0)
+            for ring in (2 * pair, 2 * pair + 1)
+        ]
         columns = slice(pair * 256, (pair + 1) * 256)
-        update = jnp.dot(low, factor, preferred_element_type=F32)
+        update = first_rows(low, jnp.concatenate(halves, axis=1))
         out[:, columns] = (keep[:, columns] + other[:, columns].astype(F32) + update).astype(BF16)
 
 
@@ -159,7 +160,7 @@
     parts = lax.all_to_all(packed, "dp", 0, 0, tiled=True)
     steps = WIDTH // TILE
     halves = pl.BlockSpec((2, TOKENS, TILE // 4), lambda step: (0, 0, step))
-    send, own, rows, row_weights = pl.pallas_call(
+    send, own, rows_t, row_weights = pl.pallas_call(
         base_kernel,
         grid=(steps,),
         in_specs=[
@@ -169,18 +170,18 @@
             whole((SLOTS, HIDDEN)),
             pl.BlockSpec((HIDDEN, TILE), lambda step: (0, step)),
         ],
-        out_specs=[halves, halves, whole((TOKENS, HIDDEN)), whole((TOKENS, 128))],
+        out_specs=[halves, halves, whole((HIDDEN, TOKENS)), whole((8, TOKENS))],
         out_shape=(
             shape((2, TOKENS, QUARTER), BF16),
             shape((2, TOKENS, QUARTER), F32),
-            shape((TOKENS, HIDDEN), BF16),
-            shape((TOKENS, 128), F32),
+            shape((HIDDEN, TOKENS), BF16),
+            shape((8, TOKENS), F32),
         ),
+        scratch_shapes=[pltpu.VMEM((TOKENS, HIDDEN), BF16), pltpu.VMEM((TOKENS, 128), F32)],
         cost_estimate=pl.CostEstimate(
             flops=2 * TOKENS * HIDDEN * WIDTH, bytes_accessed=7 * 1024 * 1024, transcendentals=0
         ),
     )(packed, expert_ids.T, combine_weights.T, slot_hidden, base_down)
-    other = lax.ppermute(send, "tensor", [(index, index ^ 1) for index in range(n_tensor)])
     new_a, new_b, spread = pl.pallas_call(
         step_kernel,
         out_shape=(
@@ -189,6 +190,8 @@
             shape((OWNERS, CHUNK, 128), BF16),
         ),
     )(parts, factor_a, moment_a, factor_b, moment_b)
+    spread, send = lax.optimization_barrier((spread, send))
+    other = lax.ppermute(send, "tensor", [(index, index ^ 1) for index in range(n_tensor)])
     gathered = lax.all_to_all(spread, "dp", 0, 0, tiled=True)
     send_low, keep = pl.pallas_call(
         middle_kernel,
@@ -199,16 +202,16 @@
     factors = lax.all_to_all(
         gathered.reshape(RING, 2 * CHUNK, 128), "tensor", 0, 0, tiled=True, axis_index_groups=rings
     )
-    packet = pl.pallas_call(
+    low = pl.pallas_call(
         low_rank_kernel,
-        out_shape=shape((64, 128), BF16),
+        out_shape=shape((RANK, TOKENS), BF16),
         scratch_shapes=[pltpu.VMEM((OWNERS * B_ROWS, RANK), F32)],
-    )(gathered, rows, row_weights)
-    packets = lax.all_gather(packet, "tensor", axis_index_groups=quads)
+    )(gathered, rows_t, row_weights)
+    lows = lax.all_gather(low, "tensor", axis_index_groups=quads)
     joined = pl.pallas_call(
         join_kernel,
         out_shape=shape((TOKENS, QUARTER), BF16),
-    )(packets, factors, keep, other_low)
+    )(lows, factors, keep, other_low)
     partials = lax.all_to_all(joined.reshape(n_tensor, 8, QUARTER), "tensor", 0, 0, tiled=True)
     scored = pl.pallas_call(
         add_kernel,

time: 99.9 us -> 95 us (0.951)
  blocking collectives: 48 us -> 33 us
  starting transfers between devices: 25.5 us -> 31.6 us
  waiting for transfers between devices: 3.7 us -> 7.51 us
    all_to_all x1 -> x0, blocking collectives: 14.3 us -> none  [body(): parts = lax.all_to_all(packed, 'dp', 0, 0, tiled=True)]
    all_to_all x0 -> x1, starting transfers between devices: none -> 10.2 us  [body(): parts = lax.all_to_all(packed, 'dp', 0, 0, tiled=True)]
    ppermute x1, starting transfers between devices: 8.79 us -> 4.64 us  [body(): lax.ppermute(send, 'tensor', [(index, index ^ 1) for index in range(n_ten...]
    all_to_all x0 -> x1, waiting for transfers between devices: none -> 3.73 us  [body(): parts = lax.all_to_all(packed, 'dp', 0, 0, tiled=True)]
  transfers between devices with their start and end apart: 4 -> 5, of which waited for: 1 -> 2; matrix products, arithmetic and copies ran while one was open for 0% -> 0% of each run, Pallas kernels for 7% -> 12%
where the time goes in v3:
time: 95 us; the launch traced here: 94.3 us
  blocking collectives  33 us (35%)
  starting transfers between devices  31.6 us (33%)
  Pallas kernels  18.9 us (20%)
  waiting for transfers between devices  7.51 us (8%)
  local copies, waits for them, and re-layouts  2.53 us (3%)
    all_to_all x1, blocking collectives, body(): lax.all_to_all(joined.reshape(n_tensor, 8, QUARTER), 'tensor', 0, 0, tile...  25.1 us
    all_to_all x1, starting transfers between devices, body(): parts = lax.all_to_all(packed, 'dp', 0, 0, tiled=True)  10.2 us
    all_to_all x1, starting transfers between devices, body(): lax.all_to_all(gathered.reshape(RING, 2 * CHUNK, 128), 'tensor', 0, 0, ti...  10 us
    all_gather x1, blocking collectives, body(): lows = lax.all_gather(low, 'tensor', axis_index_groups=quads)  7.95 us
    pallas_call x1, Pallas kernels, body(): pl.pallas_call(base_kernel, grid=(steps,), in_specs=[pl.BlockSpec(memory_...  5.91 us
    ppermute x1, starting transfers between devices, body(): lax.ppermute(send, 'tensor', [(index, index ^ 1) for index in range(n_ten...  4.64 us
    all_to_all x1, starting transfers between devices, body(): gathered = lax.all_to_all(spread, 'dp', 0, 0, tiled=True)  4.18 us
    all_to_all x1, waiting for transfers between devices, body(): gathered = lax.all_to_all(spread, 'dp', 0, 0, tiled=True)  3.78 us
  transfers between devices with their start and end apart: 5, of which 2 were waited for; matrix products, arithmetic and copies ran while one was open for 0% of the time, Pallas kernels for 12%

profile of v3, /device:TPU:1, one launch (start us, length us, event | category | flops | bytes accessed | tf_op | source)
XLA Modules:
  0.0 94.3 jit_solution(10992583522108630344)
XLA Ops:
  0.6 1.8 %shard_map.121.after = bf16[16,48,128]{2,1,0:T(8,128)(2,1)} custom-call(f32[1,512,128]{2,1,0:T(8,128)} %grad_a.1, f32[1,32,384]{2,1,0:T(8,128)} %bitcast.8), custom_call_target="tpu_custom_call" | custom-call | tf_op jit(solution)/shard_map/pallas_call | solution.py:156
  2.4 10.2 %all-to-all-start = ((bf16[16,48,128]{2,1,0:T(8,128)(2,1)}), bf16[16,48,128]{2,1,0:T(8,128)(2,1)S(1)}, u32[]{:S(2)}, u32[]{:S(2)}) async-start(bf16[16,48,128]{2,1,0:T(8,128)(2,1)} %shard_map.121.after), calls=%async_computation | async-start | bytes 393216 | tf_op jit(solution)/shard_map/all_to_all | solution.py:160
  12.7 5.9 %shard_map.123 = (bf16[2,256,1024]{2,1,0:T(8,128)(2,1)}, f32[2,256,1024]{2,1,0:T(8,128)}, bf16[384,256]{1,0:T(8,128)(2,1)}, f32[8,256]{1,0:T(8,128)}) custom-call(bf16[16,48,128]{2,1,0:T(8,128)(2,1)} %shard_map.121.after, s32[8,256]{1,0:T(8,128)} %bitcast.9, f32[8,256]{1,0:T(8,128)} %bitcast.10, bf16[192,384]{1,0:T(8,128)(2,1)} %hidden.1, bf16[384,4096]{1,0:T(8,128)(2,1)} %base.1), custom_call_target="tpu_custom_call" | custom-call | flops 805306368 | bytes 7340032 | tf_op jit(solution)/shard_map/pallas_call | solution.py:163
  18.6 3.7 %all-to-all-done.parts = bf16[16,48,128]{2,1,0:T(8,128)(2,1)S(1)} async-done(((bf16[16,48,128]{2,1,0:T(8,128)(2,1)}), bf16[16,48,128]{2,1,0:T(8,128)(2,1)S(1)}, u32[]{:S(2)}, u32[]{:S(2)}) %all-to-all-start) | async-done | bytes 196640 | tf_op jit(solution)/shard_map/all_to_all | solution.py:160
  22.3 0.0 copy-start.2
  22.3 0.7 copy-done.2
  23.0 1.8 %shard_map.122 = (f32[32,128]{1,0:T(8,128)}, f32[24,32]{1,0:T(8,128)}, bf16[16,48,128]{2,1,0:T(8,128)(2,1)}) custom-call(bf16[16,48,128]{2,1,0:T(8,128)(2,1)} %copy-done.2, f32[32,128]{1,0:T(8,128)} %factor_a.1, f32[32,128]{1,0:T(8,128)} %moment_a.1, f32[24,32]{1,0:T(8,128)} %factor_b.1, f32[24,32]{1,0:T(8,128)} %moment_b.1), custom_call_target="tpu_custom_call" | custom-call | tf_op jit(solution)/shard_map/pallas_call | solution.py:185
  24.8 4.6 %collective-permute-start = (bf16[2,256,1024]{2,1,0:T(8,128)(2,1)}, bf16[2,256,1024]{2,1,0:T(8,128)(2,1)S(1)}, u32[]{:S(2)}, u32[]{:S(2)}) collective-permute-start(bf16[2,256,1024]{2,1,0:T(8,128)(2,1)} %get-tuple-element.22), channel_id=1, source_target_pairs={{0,1},{1,0},{2,3},{3,2},{4,5},{5,4},{6,7},{7,6},{8,9},{9,8},{10,11... | collective-permute-start | bytes 3145736 | tf_op jit(solution)/shard_map/ppermute | solution.py:194
  29.4 4.2 %all-to-all-start.1 = ((bf16[16,48,128]{2,1,0:T(8,128)(2,1)}), bf16[16,48,128]{2,1,0:T(8,128)(2,1)}, u32[]{:S(2)}, u32[]{:S(2)}) async-start(bf16[16,48,128]{2,1,0:T(8,128)(2,1)} %get-tuple-element.18), calls=%async_computation.1 | async-start | bytes 393216 | tf_op jit(solution)/shard_map/all_to_all | solution.py:195
  33.6 0.0 collective-permute-done.other
  33.6 0.0 copy-start
  33.7 1.0 %copy-done = bf16[2,256,1024]{2,1,0:T(8,128)(2,1)} copy-done((bf16[2,256,1024]{2,1,0:T(8,128)(2,1)}, bf16[2,256,1024]{2,1,0:T(8,128)(2,1)S(1)}, u32[]{:S(2)}) %copy-start) | copy-done | bytes 1048600
  34.6 3.2 %shard_map.125 = (bf16[256,1024]{1,0:T(8,128)(2,1)}, f32[256,1024]{1,0:T(8,128)}) custom-call(f32[2,256,1024]{2,1,0:T(8,128)} %get-tuple-element.21.own, bf16[2,256,1024]{2,1,0:T(8,128)(2,1)} %copy-done), custom_call_target="tpu_custom_call" | custom-call | flops 1048576 | bytes 4194304 | tf_op jit(solution)/shard_map/pallas_call | solution.py:196
  37.8 2.5 %collective-permute-start.1 = (bf16[256,1024]{1,0:T(8,128)(2,1)}, bf16[256,1024]{1,0:T(8,128)(2,1)S(1)}, u32[]{:S(2)}, u32[]{:S(2)}) collective-permute-start(bf16[256,1024]{1,0:T(8,128)(2,1)} %get-tuple-element.24), channel_id=1, source_target_pairs={{0,2},{1,3},{2,0},{3,1},{4,6},{5,7},{6,4},{7,5},{8,10},{9,11},{10,... | collective-permute-start | bytes 1572872 | tf_op jit(solution)/shard_map/ppermute | solution.py:201
  40.3 3.8 %all-to-all-done.1.gathered = bf16[16,48,128]{2,1,0:T(8,128)(2,1)} async-done(((bf16[16,48,128]{2,1,0:T(8,128)(2,1)}), bf16[16,48,128]{2,1,0:T(8,128)(2,1)}, u32[]{:S(2)}, u32[]{:S(2)}) %all-to-all-start.1) | async-done | bytes 196640 | tf_op jit(solution)/shard_map/all_to_all | solution.py:195
  44.1 10.0 %all-to-all-start.2 = ((bf16[8,96,128]{2,1,0:T(8,128)(2,1)}), bf16[8,96,128]{2,1,0:T(8,128)(2,1)S(1)}, u32[]{:S(2)}, u32[]{:S(2)}) async-start(bf16[8,96,128]{2,1,0:T(8,128)(2,1)} %bitcast.4), calls=%async_computation.2 | async-start | bytes 393216 | tf_op jit(solution)/shard_map/all_to_all | solution.py:202
  54.1 1.9 %shard_map.124 = bf16[32,256]{1,0:T(8,128)(2,1)} custom-call(bf16[16,48,128]{2,1,0:T(8,128)(2,1)} %all-to-all-done.1.gathered, bf16[384,256]{1,0:T(8,128)(2,1)} %get-tuple-element.19.rows_t, f32[8,256]{1,0:T(8,128)} %get-tuple-element.20.row_weights), custom_call_target="tpu_custom_call" | custom-call | tf_op jit(solution)/shard_map/pallas_call | solution.py:205
  56.0 8.0 %all-gather = bf16[128,256]{1,0:T(8,128)(2,1)} all-gather(bf16[32,256]{1,0:T(8,128)(2,1)} %shard_map.124), channel_id=2, replica_groups={{0,1,2,3},{4,5,6,7},{8,9,10,11},{12,13,14,15},{16,17,18,19},{20,21,22,2..., dimensions={0}, use_global_device_ids=true | all-gather | bytes 81920 | tf_op jit(solution)/shard_map/all_gather | solution.py:210
  64.0 0.0 all-to-all-done.2.factors
  64.0 0.0 copy-start.1
  64.0 0.0 collective-permute-done.1.other
  64.0 0.0 copy-start.3
  64.0 0.7 copy-done.1
  64.7 0.2 copy-done.3
  64.8 2.6 %shard_map.126 = bf16[256,1024]{1,0:T(8,128)(2,1)} custom-call(bf16[4,32,256]{2,1,0:T(8,128)(2,1)} %bitcast.7, bf16[8,96,128]{2,1,0:T(8,128)(2,1)} %copy-done.1, f32[256,1024]{1,0:T(8,128)} %get-tuple-element.23.keep, bf16[256,1024]{1,0:T(8,128)(2,1)} %copy-done.3), custom_call_target="tpu_custom_call" | custom-call | tf_op jit(solution)/shard_map/pallas_call | solution.py:211
  67.5 25.1 %all_to_all.20.parts = bf16[32,8,1024]{2,1,0:T(8,128)(2,1)} all-to-all(bf16[32,8,1024]{2,1,0:T(8,128)(2,1)} %bitcast.6), channel_id=1, replica_groups=mesh['dp'=16,'tensor'=32] {'tensor'}, dimensions={0} | all-to-all | bytes 1048576 | tf_op jit(solution)/shard_map/all_to_all | solution.py:215
  92.5 1.7 %shard_map.127 = bf16[8,4096]{1,0:T(8,128)(2,1)} custom-call(bf16[32,8,1024]{2,1,0:T(8,128)(2,1)} %all_to_all.20.parts), custom_call_target="tpu_custom_call" | custom-call | tf_op jit(solution)/shard_map/pallas_call | solution.py:216
Async XLA Ops:
  2.4 19.9 %all-to-all-start = ((bf16[16,48,128]{2,1,0:T(8,128)(2,1)}), bf16[16,48,128]{2,1,0:T(8,128)(2,1)S(1)}, u32[]{:S(2)}, u32[]{:S(2)}) async-start(bf16[16,48,128]{2,1,0:T(8,128)(2,1)} %shard_map.121.after), calls=%async_computation | async-start | bytes 393216 | tf_op jit(solution)/shard_map/all_to_all | solution.py:160
  22.3 0.7 copy-start.2
  24.8 8.8 %collective-permute-start = (bf16[2,256,1024]{2,1,0:T(8,128)(2,1)}, bf16[2,256,1024]{2,1,0:T(8,128)(2,1)S(1)}, u32[]{:S(2)}, u32[]{:S(2)}) collective-permute-start(bf16[2,256,1024]{2,1,0:T(8,128)(2,1)} %get-tuple-element.22), channel_id=1, source_target_pairs={{0,1},{1,0},{2,3},{3,2},{4,5},{5,4},{6,7},{7,6},{8,9},{9,8},{10,11... | collective-permute-start | bytes 3145736 | tf_op jit(solution)/shard_map/ppermute | solution.py:194
  29.4 14.6 %all-to-all-start.1 = ((bf16[16,48,128]{2,1,0:T(8,128)(2,1)}), bf16[16,48,128]{2,1,0:T(8,128)(2,1)}, u32[]{:S(2)}, u32[]{:S(2)}) async-start(bf16[16,48,128]{2,1,0:T(8,128)(2,1)} %get-tuple-element.18), calls=%async_computation.1 | async-start | bytes 393216 | tf_op jit(solution)/shard_map/all_to_all | solution.py:195
  33.6 1.0 %copy-start = (bf16[2,256,1024]{2,1,0:T(8,128)(2,1)}, bf16[2,256,1024]{2,1,0:T(8,128)(2,1)S(1)}, u32[]{:S(2)}) copy-start(bf16[2,256,1024]{2,1,0:T(8,128)(2,1)S(1)} %collective-permute-done.other) | copy-start | bytes 3145732
  37.8 26.2 %collective-permute-start.1 = (bf16[256,1024]{1,0:T(8,128)(2,1)}, bf16[256,1024]{1,0:T(8,128)(2,1)S(1)}, u32[]{:S(2)}, u32[]{:S(2)}) collective-permute-start(bf16[256,1024]{1,0:T(8,128)(2,1)} %get-tuple-element.24), channel_id=1, source_target_pairs={{0,2},{1,3},{2,0},{3,1},{4,6},{5,7},{6,4},{7,5},{8,10},{9,11},{10,... | collective-permute-start | bytes 1572872 | tf_op jit(solution)/shard_map/ppermute | solution.py:201
  44.1 19.9 %all-to-all-start.2 = ((bf16[8,96,128]{2,1,0:T(8,128)(2,1)}), bf16[8,96,128]{2,1,0:T(8,128)(2,1)S(1)}, u32[]{:S(2)}, u32[]{:S(2)}) async-start(bf16[8,96,128]{2,1,0:T(8,128)(2,1)} %bitcast.4), calls=%async_computation.2 | async-start | bytes 393216 | tf_op jit(solution)/shard_map/all_to_all | solution.py:202
  64.0 0.7 copy-start.1
  64.0 0.9 copy-start.3

commit v4 on v3

--- a/solution.py
+++ b/solution.py
@@ -39,18 +39,23 @@
         out[owner, RANK:CHUNK, :] = pack_b(block).astype(BF16)
 
 
-def step_kernel(parts, factor_a, moment_a, factor_b, moment_b, new_a, new_b, spread):
+def step_kernel(parts, factor_a, moment_a, factor_b, moment_b, sum_a, sum_b, spread):
     total = parts[0].astype(F32)
     for owner in range(1, OWNERS):
         total = total + parts[owner].astype(F32)
     stepped_a = factor_a[...] - RATE * (MOMENTUM * moment_a[...] + total[0:RANK])
     grad_b = jnp.concatenate([total[RANK:CHUNK, 0:32], total[RANK : RANK + 8, 32:64]], axis=0)
     stepped_b = factor_b[...] - RATE * (MOMENTUM * moment_b[...] + grad_b)
-    new_a[...] = stepped_a
-    new_b[...] = stepped_b
+    sum_a[...] = total[0:RANK]
+    sum_b[...] = grad_b
     chunk = jnp.concatenate([stepped_a, pack_b(stepped_b)], axis=0).astype(BF16)
     for owner in range(OWNERS):
         spread[owner] = chunk
+
+
+def output_kernel(sum_a, sum_b, factor_a, moment_a, factor_b, moment_b, new_a, new_b):
+    new_a[...] = factor_a[...] - RATE * (MOMENTUM * moment_a[...] + sum_a[...])
+    new_b[...] = factor_b[...] - RATE * (MOMENTUM * moment_b[...] + sum_b[...])
 
 
 def base_kernel(after, ids, weights, hidden, base, send, own, rows_t, row_weights, rows, column):
@@ -155,6 +160,7 @@
     rings = [[4 * ring + part for ring in range(n_tensor // 4)] for part in range(4)]
     packed = pl.pallas_call(
         pack_kernel,
+        compiler_params=pltpu.CompilerParams(vmem_limit_bytes=4 * 2**20),
         out_shape=shape((OWNERS, CHUNK, 128), BF16),
     )(grad_a_parts, jnp.swapaxes(grad_b_parts, 1, 2))
     parts = lax.all_to_all(packed, "dp", 0, 0, tiled=True)
@@ -162,6 +168,7 @@
     halves = pl.BlockSpec((2, TOKENS, TILE // 4), lambda step: (0, 0, step))
     send, own, rows_t, row_weights = pl.pallas_call(
         base_kernel,
+        compiler_params=pltpu.CompilerParams(vmem_limit_bytes=16 * 2**20),
         grid=(steps,),
         in_specs=[
             pl.BlockSpec(memory_space=pl.ANY),
@@ -182,8 +189,9 @@
             flops=2 * TOKENS * HIDDEN * WIDTH, bytes_accessed=7 * 1024 * 1024, transcendentals=0
         ),
     )(packed, expert_ids.T, combine_weights.T, slot_hidden, base_down)
-    new_a, new_b, spread = pl.pallas_call(
+    sum_a, sum_b, spread = pl.pallas_call(
         step_kernel,
+        compiler_params=pltpu.CompilerParams(vmem_limit_bytes=4 * 2**20),
         out_shape=(
             shape((RANK, 128), F32),
             shape((B_ROWS, RANK), F32),
@@ -193,8 +201,16 @@
     spread, send = lax.optimization_barrier((spread, send))
     other = lax.ppermute(send, "tensor", [(index, index ^ 1) for index in range(n_tensor)])
     gathered = lax.all_to_all(spread, "dp", 0, 0, tiled=True)
+    new_a, new_b = pl.pallas_call(
+        output_kernel,
+        compiler_params=pltpu.CompilerParams(vmem_limit_bytes=2 * 2**20),
+        out_shape=(shape((RANK, 128), F32), shape((B_ROWS, RANK), F32)),
+        cost_estimate=pl.CostEstimate(flops=2**34, bytes_accessed=2**17, transcendentals=0),
+    )(sum_a, sum_b, factor_a, moment_a, factor_b, moment_b)
+    own, new_a, new_b = lax.optimization_barrier((own, new_a, new_b))
     send_low, keep = pl.pallas_call(
         middle_kernel,
+        compiler_params=pltpu.CompilerParams(vmem_limit_bytes=12 * 2**20),
         out_shape=(shape((TOKENS, QUARTER), BF16), shape((TOKENS, QUARTER), F32)),
         cost_estimate=pl.CostEstimate(flops=2**20, bytes_accessed=4 * 2**20, transcendentals=0),
     )(own, other)
@@ -204,17 +220,20 @@
     )
     low = pl.pallas_call(
         low_rank_kernel,
+        compiler_params=pltpu.CompilerParams(vmem_limit_bytes=4 * 2**20),
         out_shape=shape((RANK, TOKENS), BF16),
         scratch_shapes=[pltpu.VMEM((OWNERS * B_ROWS, RANK), F32)],
     )(gathered, rows_t, row_weights)
     lows = lax.all_gather(low, "tensor", axis_index_groups=quads)
     joined = pl.pallas_call(
         join_kernel,
+        compiler_params=pltpu.CompilerParams(vmem_limit_bytes=8 * 2**20),
         out_shape=shape((TOKENS, QUARTER), BF16),
     )(lows, factors, keep, other_low)
     partials = lax.all_to_all(joined.reshape(n_tensor, 8, QUARTER), "tensor", 0, 0, tiled=True)
     scored = pl.pallas_call(
         add_kernel,
+        compiler_params=pltpu.CompilerParams(vmem_limit_bytes=4 * 2**20),
         out_shape=shape((8, WIDTH), BF16),
     )(partials)
     return new_a, new_b, scored

time: 95 us -> 87.2 us (0.918)
  Pallas kernels: 18.9 us -> 8.77 us
  local copies, waits for them, and re-layouts: 2.53 us -> 6.94 us
  waiting for transfers between devices: 7.51 us -> 3.58 us
  starting transfers between devices: 31.6 us -> 33.9 us
    pallas_call x7 -> x8, Pallas kernels: 18.9 us -> 8.77 us  [the longest x1 3.24 us: body(): pl.pallas_call(base_kernel, compiler_params=pltpu.CompilerParams(vmem_lim...]
    unnamed x8 -> x22, local copies, waits for them, and re-layouts: 2.53 us -> 6.94 us
    all_to_all x1, starting transfers between devices: 4.18 us -> 7.92 us  [body(): gathered = lax.all_to_all(spread, 'dp', 0, 0, tiled=True)]
    all_to_all x1, waiting for transfers between devices: 3.78 us -> 0.52 us  [body(): gathered = lax.all_to_all(spread, 'dp', 0, 0, tiled=True)]
    all_to_all x1, waiting for transfers between devices: 3.73 us -> 1.19 us  [body(): parts = lax.all_to_all(packed, 'dp', 0, 0, tiled=True)]
    ppermute x1, waiting for transfers between devices: 0.01 us -> 1.86 us  [body(): lax.ppermute(send, 'tensor', [(index, index ^ 1) for index in range(n_ten...]
    ppermute x1, starting transfers between devices: 4.64 us -> 3.39 us  [body(): lax.ppermute(send, 'tensor', [(index, index ^ 1) for index in range(n_ten...]
  transfers between devices with their start and end apart: 5 -> 5, of which waited for: 2 -> 3; matrix products, arithmetic and copies ran while one was open for 0% -> 0% of each run, Pallas kernels for 12% -> 7%
where the time goes in v4:
time: 87.2 us; the launch traced here: 86.5 us
  starting transfers between devices  33.9 us (39%)
  blocking collectives  32.6 us (37%)
  Pallas kernels  8.77 us (10%)
  local copies, waits for them, and re-layouts  6.94 us (8%)
  waiting for transfers between devices  3.58 us (4%)
    all_to_all x1, blocking collectives, body(): lax.all_to_all(joined.reshape(n_tensor, 8, QUARTER), 'tensor', 0, 0, tile...  24.2 us
    all_to_all x1, starting transfers between devices, body(): parts = lax.all_to_all(packed, 'dp', 0, 0, tiled=True)  10.2 us
    all_to_all x1, starting transfers between devices, body(): lax.all_to_all(gathered.reshape(RING, 2 * CHUNK, 128), 'tensor', 0, 0, ti...  10 us
    all_gather x1, blocking collectives, body(): lows = lax.all_gather(low, 'tensor', axis_index_groups=quads)  8.41 us
    all_to_all x1, starting transfers between devices, body(): gathered = lax.all_to_all(spread, 'dp', 0, 0, tiled=True)  7.92 us
    unnamed x22, local copies, waits for them, and re-layouts  6.94 us
    ppermute x1, starting transfers between devices, body(): lax.ppermute(send, 'tensor', [(index, index ^ 1) for index in range(n_ten...  3.39 us
    pallas_call x1, Pallas kernels, body(): pl.pallas_call(base_kernel, compiler_params=pltpu.CompilerParams(vmem_lim...  3.24 us
  transfers between devices with their start and end apart: 5, of which 3 were waited for; matrix products, arithmetic and copies ran while one was open for 0% of the time, Pallas kernels for 7%

profile of v4, /device:TPU:1, one launch (start us, length us, event | category | flops | bytes accessed | tf_op | source)
XLA Modules:
  0.0 86.5 jit_solution(7408388490846876291)
XLA Ops:
  0.6 0.0 copy-start.1
  0.6 0.9 %copy-done.1 = f32[1,512,128]{2,1,0:T(8,128)S(1)} copy-done((f32[1,512,128]{2,1,0:T(8,128)S(1)}, f32[1,512,128]{2,1,0:T(8,128)}, u32[]{:S(2)}) %copy-start.1) | copy-done | bytes 262168
  1.6 0.0 copy-start.3
  1.6 0.8 copy-done.3
  2.4 0.0 copy-start.4
  2.4 0.0 copy-start.5
  2.4 0.0 copy-start.6
  2.4 0.0 copy-start.7
  2.4 0.9 shard_map.121.after
  3.2 10.2 %all-to-all-start = ((bf16[16,48,128]{2,1,0:T(8,128)(2,1)}), bf16[16,48,128]{2,1,0:T(8,128)(2,1)S(1)}, u32[]{:S(2)}, u32[]{:S(2)}) async-start(bf16[16,48,128]{2,1,0:T(8,128)(2,1)} %shard_map.121.after), calls=%async_computation | async-start | bytes 393216 | tf_op jit(solution)/shard_map/all_to_all | solution.py:166
  13.5 0.0 copy-start
  13.5 1.9 %copy-done = bf16[384,4096]{1,0:T(8,128)(2,1)S(1)} copy-done((bf16[384,4096]{1,0:T(8,128)(2,1)S(1)}, bf16[384,4096]{1,0:T(8,128)(2,1)}, u32[]{:S(2)}) %copy-start) | copy-done | bytes 3145752
  15.4 0.0 copy-start.2
  15.4 0.9 %copy-done.2 = bf16[192,384]{1,0:T(8,128)(2,1)S(1)} copy-done((bf16[192,384]{1,0:T(8,128)(2,1)S(1)}, bf16[192,384]{1,0:T(8,128)(2,1)}, u32[]{:S(2)}) %copy-start.2) | copy-done | bytes 147480
  16.3 0.0 copy-start.8
  16.3 0.7 copy-done.8
  17.0 0.0 copy-start.9
  17.0 0.7 copy-done.9
  17.7 3.2 %shard_map.122 = (bf16[2,256,1024]{2,1,0:T(8,128)(2,1)S(1)}, f32[2,256,1024]{2,1,0:T(8,128)S(1)}, bf16[384,256]{1,0:T(8,128)(2,1)S(1)}, f32[8,256]{1,0:T(8,128)S(1)}) custom-call(bf16[16,48,128]{2,1,0:T(8,128)(2,1)} %shard_map.121.after, s32[8,256]{1,0:T(8,128)S(1)} %bitcast.9, f32[8,256]{1,0:T(8,128)S(1)} %bitcast.10, bf16[192,384]{1,0:T(8,128)(2,1)S(1)} %copy-done.2, ...), custom_call_target="tpu_custom_call" | custom-call | flops 805306368 | bytes 7340032 | tf_op jit(solution)/shard_map/pallas_call | solution.py:169
  20.9 0.0 copy-start.10
  20.9 1.0 %copy-done.10 = bf16[2,256,1024]{2,1,0:T(8,128)(2,1)} copy-done((bf16[2,256,1024]{2,1,0:T(8,128)(2,1)}, bf16[2,256,1024]{2,1,0:T(8,128)(2,1)S(1)}, u32[]{:S(2)}) %copy-start.10) | copy-done | bytes 1048600
  21.9 1.2 %all-to-all-done.parts = bf16[16,48,128]{2,1,0:T(8,128)(2,1)S(1)} async-done(((bf16[16,48,128]{2,1,0:T(8,128)(2,1)}), bf16[16,48,128]{2,1,0:T(8,128)(2,1)S(1)}, u32[]{:S(2)}, u32[]{:S(2)}) %all-to-all-start) | async-done | bytes 196640 | tf_op jit(solution)/shard_map/all_to_all | solution.py:166
  23.1 0.0 copy-done.4
  23.1 0.0 copy-done.5
  23.1 0.0 copy-done.6
  23.1 0.0 copy-done.7
  23.1 0.9 shard_map.123
  24.0 7.9 %all-to-all-start.1 = ((bf16[16,48,128]{2,1,0:T(8,128)(2,1)}), bf16[16,48,128]{2,1,0:T(8,128)(2,1)}, u32[]{:S(2)}, u32[]{:S(2)}) async-start(bf16[16,48,128]{2,1,0:T(8,128)(2,1)} %get-tuple-element.28), calls=%async_computation.1 | async-start | bytes 393216 | tf_op jit(solution)/shard_map/all_to_all | solution.py:203
  31.9 3.4 %collective-permute-start = (bf16[2,256,1024]{2,1,0:T(8,128)(2,1)}, bf16[2,256,1024]{2,1,0:T(8,128)(2,1)S(1)}, u32[]{:S(2)}, u32[]{:S(2)}) collective-permute-start(bf16[2,256,1024]{2,1,0:T(8,128)(2,1)} %copy-done.10), channel_id=1, source_target_pairs={{0,1},{1,0},{2,3},{3,2},{4,5},{5,4},{6,7},{7,6},{8,9},{9,8},{10,11... | collective-permute-start | bytes 3145736 | tf_op jit(solution)/shard_map/ppermute | solution.py:202
  35.3 0.6 shard_map.124
  35.9 1.9 %collective-permute-done.other = bf16[2,256,1024]{2,1,0:T(8,128)(2,1)S(1)} collective-permute-done((bf16[2,256,1024]{2,1,0:T(8,128)(2,1)}, bf16[2,256,1024]{2,1,0:T(8,128)(2,1)S(1)}, u32[]{:S(2)}, u32[]{:S(2)}) %collective-permute-start) | collective-permute-done | bytes 1048608 | tf_op jit(solution)/shard_map/ppermute | solution.py:202
  37.8 1.0 %shard_map.126 = (bf16[256,1024]{1,0:T(8,128)(2,1)}, f32[256,1024]{1,0:T(8,128)S(1)}) custom-call(f32[2,256,1024]{2,1,0:T(8,128)S(1)} %get-tuple-element.31.own, bf16[2,256,1024]{2,1,0:T(8,128)(2,1)S(1)} %collective-permute-done.other), custom_call_target="tpu_custom_call" | custom-call | flops 1048576 | bytes 4194304 | tf_op jit(solution)/shard_map/pallas_call | solution.py:211
  38.7 2.3 %collective-permute-start.1 = (bf16[256,1024]{1,0:T(8,128)(2,1)}, bf16[256,1024]{1,0:T(8,128)(2,1)S(1)}, u32[]{:S(2)}, u32[]{:S(2)}) collective-permute-start(bf16[256,1024]{1,0:T(8,128)(2,1)} %get-tuple-element.34), channel_id=1, source_target_pairs={{0,2},{1,3},{2,0},{3,1},{4,6},{5,7},{6,4},{7,5},{8,10},{9,11},{10,... | collective-permute-start | bytes 1572872 | tf_op jit(solution)/shard_map/ppermute | solution.py:217
  41.0 0.5 all-to-all-done.1.gathered
  41.6 10.0 %all-to-all-start.2 = ((bf16[8,96,128]{2,1,0:T(8,128)(2,1)}), bf16[8,96,128]{2,1,0:T(8,128)(2,1)S(1)}, u32[]{:S(2)}, u32[]{:S(2)}) async-start(bf16[8,96,128]{2,1,0:T(8,128)(2,1)} %bitcast.4), calls=%async_computation.2 | async-start | bytes 393216 | tf_op jit(solution)/shard_map/all_to_all | solution.py:218
  51.6 1.2 %shard_map.125 = bf16[32,256]{1,0:T(8,128)(2,1)S(1)} custom-call(bf16[16,48,128]{2,1,0:T(8,128)(2,1)} %all-to-all-done.1.gathered, bf16[384,256]{1,0:T(8,128)(2,1)S(1)} %get-tuple-element.29.rows_t, f32[8,256]{1,0:T(8,128)S(1)} %get-tuple-element.30.row_weights), custom_call_target="tpu_custom_call" | custom-call | tf_op jit(solution)/shard_map/pallas_call | solution.py:221
  52.8 8.4 %all-gather = bf16[128,256]{1,0:T(8,128)(2,1)S(1)} all-gather(bf16[32,256]{1,0:T(8,128)(2,1)S(1)} %shard_map.125), channel_id=2, replica_groups={{0,1,2,3},{4,5,6,7},{8,9,10,11},{12,13,14,15},{16,17,18,19},{20,21,22,2..., dimensions={0}, use_global_device_ids=true | all-gather | bytes 81920 | tf_op jit(solution)/shard_map/all_gather | solution.py:227
  61.2 0.0 all-to-all-done.2.factors
  61.2 0.0 collective-permute-done.1.other
  61.3 0.3 shard_map.127
  61.6 24.2 %all_to_all.20.parts = bf16[32,8,1024]{2,1,0:T(8,128)(2,1)S(1)} all-to-all(bf16[32,8,1024]{2,1,0:T(8,128)(2,1)S(1)} %bitcast.6), channel_id=1, replica_groups=mesh['dp'=16,'tensor'=32] {'tensor'}, dimensions={0} | all-to-all | bytes 1048576 | tf_op jit(solution)/shard_map/all_to_all | solution.py:233
  85.8 0.7 shard_map.128
Async XLA Ops:
  0.6 1.0 %copy-start.1 = (f32[1,512,128]{2,1,0:T(8,128)S(1)}, f32[1,512,128]{2,1,0:T(8,128)}, u32[]{:S(2)}) copy-start(f32[1,512,128]{2,1,0:T(8,128)} %grad_a.1) | copy-start | bytes 786436
  1.6 0.8 copy-start.3
  2.4 20.7 %copy-start.4 = (f32[32,128]{1,0:T(8,128)S(1)}, f32[32,128]{1,0:T(8,128)}, u32[]{:S(2)}) copy-start(f32[32,128]{1,0:T(8,128)} %factor_a.3) | copy-start | bytes 49156
  2.4 20.7 %copy-start.5 = (f32[32,128]{1,0:T(8,128)S(1)}, f32[32,128]{1,0:T(8,128)}, u32[]{:S(2)}) copy-start(f32[32,128]{1,0:T(8,128)} %moment_a.3) | copy-start | bytes 49156
  2.4 20.7 %copy-start.6 = (f32[24,32]{1,0:T(8,128)S(1)}, f32[24,32]{1,0:T(8,128)}, u32[]{:S(2)}) copy-start(f32[24,32]{1,0:T(8,128)} %factor_b.3) | copy-start | bytes 9220
  2.4 20.7 %copy-start.7 = (f32[24,32]{1,0:T(8,128)S(1)}, f32[24,32]{1,0:T(8,128)}, u32[]{:S(2)}) copy-start(f32[24,32]{1,0:T(8,128)} %moment_b.3) | copy-start | bytes 9220
  3.2 19.9 %all-to-all-start = ((bf16[16,48,128]{2,1,0:T(8,128)(2,1)}), bf16[16,48,128]{2,1,0:T(8,128)(2,1)S(1)}, u32[]{:S(2)}, u32[]{:S(2)}) async-start(bf16[16,48,128]{2,1,0:T(8,128)(2,1)} %shard_map.121.after), calls=%async_computation | async-start | bytes 393216 | tf_op jit(solution)/shard_map/all_to_all | solution.py:166
  13.5 1.9 %copy-start = (bf16[384,4096]{1,0:T(8,128)(2,1)S(1)}, bf16[384,4096]{1,0:T(8,128)(2,1)}, u32[]{:S(2)}) copy-start(bf16[384,4096]{1,0:T(8,128)(2,1)} %base.1) | copy-start | bytes 9437188
  15.4 0.9 %copy-start.2 = (bf16[192,384]{1,0:T(8,128)(2,1)S(1)}, bf16[192,384]{1,0:T(8,128)(2,1)}, u32[]{:S(2)}) copy-start(bf16[192,384]{1,0:T(8,128)(2,1)} %hidden.1) | copy-start | bytes 442372
  16.3 0.7 copy-start.8
  17.0 0.7 copy-start.9
  20.9 1.0 %copy-start.10 = (bf16[2,256,1024]{2,1,0:T(8,128)(2,1)}, bf16[2,256,1024]{2,1,0:T(8,128)(2,1)S(1)}, u32[]{:S(2)}) copy-start(bf16[2,256,1024]{2,1,0:T(8,128)(2,1)S(1)} %get-tuple-element.32) | copy-start | bytes 3145732
  24.0 17.6 %all-to-all-start.1 = ((bf16[16,48,128]{2,1,0:T(8,128)(2,1)}), bf16[16,48,128]{2,1,0:T(8,128)(2,1)}, u32[]{:S(2)}, u32[]{:S(2)}) async-start(bf16[16,48,128]{2,1,0:T(8,128)(2,1)} %get-tuple-element.28), calls=%async_computation.1 | async-start | bytes 393216 | tf_op jit(solution)/shard_map/all_to_all | solution.py:203
  31.9 5.9 %collective-permute-start = (bf16[2,256,1024]{2,1,0:T(8,128)(2,1)}, bf16[2,256,1024]{2,1,0:T(8,128)(2,1)S(1)}, u32[]{:S(2)}, u32[]{:S(2)}) collective-permute-start(bf16[2,256,1024]{2,1,0:T(8,128)(2,1)} %copy-done.10), channel_id=1, source_target_pairs={{0,1},{1,0},{2,3},{3,2},{4,5},{5,4},{6,7},{7,6},{8,9},{9,8},{10,11... | collective-permute-start | bytes 3145736 | tf_op jit(solution)/shard_map/ppermute | solution.py:202
  38.7 22.5 %collective-permute-start.1 = (bf16[256,1024]{1,0:T(8,128)(2,1)}, bf16[256,1024]{1,0:T(8,128)(2,1)S(1)}, u32[]{:S(2)}, u32[]{:S(2)}) collective-permute-start(bf16[256,1024]{1,0:T(8,128)(2,1)} %get-tuple-element.34), channel_id=1, source_target_pairs={{0,2},{1,3},{2,0},{3,1},{4,6},{5,7},{6,4},{7,5},{8,10},{9,11},{10,... | collective-permute-start | bytes 1572872 | tf_op jit(solution)/shard_map/ppermute | solution.py:217
  41.6 19.7 %all-to-all-start.2 = ((bf16[8,96,128]{2,1,0:T(8,128)(2,1)}), bf16[8,96,128]{2,1,0:T(8,128)(2,1)S(1)}, u32[]{:S(2)}, u32[]{:S(2)}) async-start(bf16[8,96,128]{2,1,0:T(8,128)(2,1)} %bitcast.4), calls=%async_computation.2 | async-start | bytes 393216 | tf_op jit(solution)/shard_map/all_to_all | solution.py:218

commit v5 on v3

v5 whole, which is shorter than its diff:
```python
import jax
import jax.numpy as jnp
from jax import lax
from jax.experimental import pallas as pl
from jax.experimental.pallas import tpu as pltpu
from jax.sharding import PartitionSpec as P

MOMENTUM = 0.9
RATE = 0.5
RANK = 32
B_ROWS = 24
CHUNK = 48
OWNERS = 16
CHIPS = 16
SLOTS = 192
TOKENS = 256
HIDDEN = 384
WIDTH = 4096
SETS = 8
SET_WIDTH = 512
PAIR_WIDTH = 256
F32 = jnp.float32
BF16 = jnp.bfloat16


def pack_b(block):
    tail = jnp.concatenate([block[16:24], jnp.zeros((8, RANK), F32)], axis=0)
    return jnp.concatenate([block[0:16], tail, jnp.zeros((16, 64), F32)], axis=1)


def first_rows(a, b):
    return lax.dot_general(a, b, (((0,), (0,)), ((), ())), preferred_element_type=F32)


def pack_kernel(grad_a, grad_b, out):
    columns = grad_b[0].T
    for owner in range(OWNERS):
        out[owner, 0:RANK, :] = grad_a[0, owner * RANK : (owner + 1) * RANK, :].astype(BF16)
        block = columns[owner * B_ROWS : (owner + 1) * B_ROWS, :]
        out[owner, RANK:CHUNK, :] = pack_b(block).astype(BF16)


def step_kernel(parts, factor_a, moment_a, factor_b, moment_b, sum_a, sum_b, spread):
    total = parts[0].astype(F32)
    for owner in range(1, OWNERS):
        total = total + parts[owner].astype(F32)
    stepped_a = factor_a[...] - RATE * (MOMENTUM * moment_a[...] + total[0:RANK])
    grad_b = jnp.concatenate([total[RANK:CHUNK, 0:32], total[RANK : RANK + 8, 32:64]], axis=0)
    stepped_b = factor_b[...] - RATE * (MOMENTUM * moment_b[...] + grad_b)
    sum_a[...] = total[0:RANK]
    sum_b[...] = grad_b
    chunk = jnp.concatenate([stepped_a, pack_b(stepped_b)], axis=0).astype(BF16)
    for owner in range(OWNERS):
        spread[owner] = chunk


def output_kernel(sum_a, sum_b, factor_a, moment_a, factor_b, moment_b, new_a, new_b):
    new_a[...] = factor_a[...] - RATE * (MOMENTUM * moment_a[...] + sum_a[...])
    new_b[...] = factor_b[...] - RATE * (MOMENTUM * moment_b[...] + sum_b[...])


def base_kernel(after, ids, weights, hidden, base, send, own, rows_t, row_weights, rows, column):
    index = lax.axis_index("tensor")
    expert, core = index // 2, index % 2
    named = ids[...] == expert
    hit = jnp.sum(jnp.where(named, 1.0, 0.0), axis=0, keepdims=True)
    weight = jnp.sum(jnp.where(named, weights[...], 0.0), axis=0, keepdims=True)
    one = lax.broadcasted_iota(jnp.int32, (TOKENS, TOKENS), 0)
    two = lax.broadcasted_iota(jnp.int32, (TOKENS, TOKENS), 1)
    earlier = jnp.where(one < two, 1.0, 0.0).astype(BF16)
    wide = jnp.broadcast_to(hit, (8, TOKENS)).astype(BF16)
    before = jnp.dot(wide, earlier, preferred_element_type=F32)[0:1]
    slot = jnp.where(hit > 0.5, before, -1.0)
    both = jnp.concatenate([slot, weight, jnp.zeros((6, TOKENS), F32)], axis=0).T
    slots = lax.broadcasted_iota(jnp.int32, (TOKENS, SLOTS), 1)
    chosen = jnp.where(both[:, 0:1].astype(jnp.int32) == slots, 1.0, 0.0).astype(BF16)
    rows[...] = jnp.dot(chosen, hidden[...], preferred_element_type=F32).astype(BF16)
    column[...] = jnp.broadcast_to(both[:, 1:2], (TOKENS, 128))
    slots_t = lax.broadcasted_iota(jnp.int32, (SLOTS, TOKENS), 0)
    chosen_t = jnp.where(slot.astype(jnp.int32) == slots_t, 1.0, 0.0).astype(BF16)
    rows_t[...] = first_rows(hidden[...], chosen_t).astype(BF16)
    row_weights[...] = jnp.broadcast_to(weight, (8, TOKENS))
    for mine in range(2):

        @pl.when(core == mine)
        def _(mine=mine):
            for place in range(4):
                for side, out in ((1 - mine, send), (mine, own)):
                    at = (2 * place + side) * SET_WIDTH
                    part = jnp.dot(rows[...], base[:, at : at + SET_WIDTH], preferred_element_type=F32)
                    out[place] = (part * column[:, 0:1]).astype(BF16)


def middle_kernel(own, other, send_1, send_2, send_3, keep):
    place = lax.axis_index("tensor") // 2 % 4
    keep[...] = own[place].astype(F32) + other[place].astype(F32)
    low = place % 2
    flipped = (place + 1 - 2 * low, (place + 2) % 4, 3 - place)
    for there, send in zip(flipped, (send_1, send_2, send_3)):
        send[...] = (own[there].astype(F32) + other[there].astype(F32)).astype(BF16)


def low_rank_kernel(gathered, rows_t, row_weights, spread, b_scr):
    for owner in range(OWNERS):
        block = gathered[owner, RANK:CHUNK, :].astype(F32)
        b_scr[owner * B_ROWS : owner * B_ROWS + 16, :] = block[:, 0:32]
        b_scr[owner * B_ROWS + 16 : (owner + 1) * B_ROWS, :] = block[0:8, 32:64]
    low = (first_rows(b_scr[...].astype(BF16), rows_t[...]) * row_weights[0:1, :]).astype(BF16)
    for chip in range(CHIPS):
        spread[chip] = low


def sum_kernel(keep, other_1, other_2, other_3, out):
    total = keep[...]
    for other in (other_1, other_2, other_3):
        total = total + other[...].astype(F32)
    out[...] = total.astype(BF16)


def join_kernel(low, factors, base, out):
    blocks = [
        jnp.concatenate([factors[0, owner, 0:RANK, :], factors[1, owner, 0:RANK, :]], axis=1)
        for owner in range(OWNERS)
    ]
    update = first_rows(low[...], jnp.concatenate(blocks, axis=0))
    out[:, 0:SET_WIDTH] = base[...]
    out[:, SET_WIDTH:] = update.astype(BF16)


def add_kernel(parts, out):
    for group in range(SETS):
        total = parts[group, :, 0:SET_WIDTH].astype(F32)
        for ring in range(1, 4):
            total = total + parts[ring * SETS + group, :, 0:SET_WIDTH].astype(F32)
        for chip in (2 * group, 2 * group + 1):
            at = chip % 2 * PAIR_WIDTH
            update = parts[2 * chip, :, SET_WIDTH:].astype(F32) + parts[2 * chip + 1, :, SET_WIDTH:].astype(F32)
            columns = slice(chip * PAIR_WIDTH, (chip + 1) * PAIR_WIDTH)
            out[:, columns] = (total[:, at : at + PAIR_WIDTH] + update).astype(BF16)


def shape(dims, dtype):
    return jax.ShapeDtypeStruct(dims, dtype)


def body(
    grad_a_parts,
    grad_b_parts,
    factor_a,
    moment_a,
    factor_b,
    moment_b,
    base_down,
    slot_hidden,
    expert_ids,
    combine_weights,
):
    n_tensor = lax.axis_size("tensor")
    pairs = [[2 * chip, 2 * chip + 1] for chip in range(n_tensor // 2)]
    same_core = [[2 * chip + core for chip in range(n_tensor // 2)] for core in range(2)]

    def swap(array, bits):
        return lax.ppermute(array, "tensor", [(index, index ^ bits) for index in range(n_tensor)])

    vmem = pl.BlockSpec(memory_space=pltpu.VMEM)

    def limit(size):
        return pltpu.CompilerParams(vmem_limit_bytes=size * 2**20)

    def cost(flops, size):
        return pl.CostEstimate(flops=flops, bytes_accessed=size, transcendentals=0)

    packed = pl.pallas_call(
        pack_kernel,
        out_shape=shape((OWNERS, CHUNK, 128), BF16),
    )(grad_a_parts, jnp.swapaxes(grad_b_parts, 1, 2))
    parts = lax.all_to_all(packed, "dp", 0, 0, tiled=True)
    send, own, rows_t, row_weights = pl.pallas_call(
        base_kernel,
        in_specs=[pl.BlockSpec(memory_space=pl.ANY), vmem, vmem, vmem, vmem],
        out_shape=(
            shape((4, TOKENS, SET_WIDTH), BF16),
            shape((4, TOKENS, SET_WIDTH), BF16),
            shape((HIDDEN, TOKENS), BF16),
            shape((8, TOKENS), F32),
        ),
        scratch_shapes=[pltpu.VMEM((TOKENS, HIDDEN), BF16), pltpu.VMEM((TOKENS, 128), F32)],
        cost_estimate=cost(2 * TOKENS * HIDDEN * WIDTH, 7 * 2**20),
    )(packed, expert_ids.T, combine_weights.T, slot_hidden, base_down)
    other = swap(send, 1)
    sum_a, sum_b, spread = pl.pallas_call(
        step_kernel,
        out_shape=(
            shape((RANK, 128), F32),
            shape((B_ROWS, RANK), F32),
            shape((OWNERS, CHUNK, 128), BF16),
        ),
        compiler_params=limit(4),
        cost_estimate=cost(2**34, 2**18),
    )(parts, factor_a, moment_a, factor_b, moment_b)
    gathered = lax.all_to_all(spread, "dp", 0, 0, tiled=True)
    flat = shape((TOKENS, SET_WIDTH), BF16)
    send_1, send_2, send_3, keep = pl.pallas_call(
        middle_kernel,
        out_shape=(flat, flat, flat, shape((TOKENS, SET_WIDTH), F32)),
        compiler_params=limit(12),
        cost_estimate=cost(2**20, 4 * 2**20),
    )(own, other)
    others = [swap(send_1, 2), swap(send_2, 4), swap(send_3, 6)]
    low_spread = pl.pallas_call(
        low_rank_kernel,
        out_shape=shape((CHIPS, RANK, TOKENS), BF16),
        scratch_shapes=[pltpu.VMEM((OWNERS * B_ROWS, RANK), F32)],
        compiler_params=limit(4),
        cost_estimate=cost(2**34, 2**18),
    )(gathered, rows_t, row_weights)
    low_spread, sum_a = lax.optimization_barrier((low_spread, sum_a))
    new_a, new_b = pl.pallas_call(
        output_kernel,
        out_shape=(shape((RANK, 128), F32), shape((B_ROWS, RANK), F32)),
        compiler_params=limit(2),
    )(sum_a, sum_b, factor_a, moment_a, factor_b, moment_b)
    low = lax.all_to_all(low_spread, "tensor", 0, 0, tiled=True, axis_index_groups=same_core)
    factors = lax.all_gather(gathered, "tensor", axis_index_groups=pairs)
    keep, new_a, new_b = lax.optimization_barrier((keep, new_a, new_b))
    base = pl.pallas_call(
        sum_kernel,
        out_shape=flat,
        compiler_params=limit(8),
        cost_estimate=cost(2**34, 2**20),
    )(keep, *others)
    joined = pl.pallas_call(
        join_kernel,
        out_shape=shape((TOKENS, SET_WIDTH + PAIR_WIDTH), BF16),
        compiler_params=limit(8),
    )(low.reshape(CHIPS * RANK, TOKENS), factors, base)
    partials = lax.all_to_all(
        joined.reshape(n_tensor, 8, SET_WIDTH + PAIR_WIDTH), "tensor", 0, 0, tiled=True
    )
    scored = pl.pallas_call(
        add_kernel,
        out_shape=shape((8, WIDTH), BF16),
        compiler_params=limit(4),
    )(partials)
    return new_a, new_b, scored


def solution(mesh):
    placed = (
        P("dp", None, "tensor"),
        P("dp", "tensor", None),
        P("dp", "tensor"),
        P("dp", "tensor"),
        P(("tensor", "dp"), None),
        P(("tensor", "dp"), None),
        P("tensor", None),
        P("dp", "tensor"),
        P("dp", None),
        P("dp", None),
    )
    return jax.shard_map(
        body,
        mesh=mesh,
        in_specs=placed,
        out_specs=(P("dp", "tensor"), P(("tensor", "dp"), None), P(("dp", "tensor"), None)),
        check_vma=False,
    )
```

time: 95 us -> 84.9 us (0.89)
  starting transfers between devices: 31.6 us -> 40.3 us
  blocking collectives: 33 us -> 24.4 us
  Pallas kernels: 18.9 us -> 11.5 us
  local copies, waits for them, and re-layouts: 2.53 us -> 0.95 us
  waiting for transfers between devices: 7.51 us -> 5.97 us
    pallas_call x5 -> x7, Pallas kernels: 15.3 us -> 8.82 us  [the longest x1 5.25 us: body(): pl.pallas_call(base_kernel, in_specs=[pl.BlockSpec(memory_space=pl.ANY),...]
    ppermute x2 -> x4, starting transfers between devices: 7.12 us -> 12 us  [swap(): lax.ppermute(array, 'tensor', [(index, index ^ bits) for index in range(n...]
    all_to_all x1, blocking collectives: 25.1 us -> 20.4 us  [body(): lax.all_to_all(joined.reshape(n_tensor, 8, SET_WIDTH + PAIR_WIDTH), 'tens...]
    all_to_all x1, waiting for transfers between devices: 0.01 us -> 4.11 us  [body(): lax.all_to_all(low_spread, 'tensor', 0, 0, tiled=True, axis_index_groups=...]
    all_gather x1, blocking collectives: 7.95 us -> 3.98 us  [body(): factors = lax.all_gather(gathered, 'tensor', axis_index_groups=pairs)]
    all_to_all x1, starting transfers between devices: 4.18 us -> 7.96 us  [body(): gathered = lax.all_to_all(spread, 'dp', 0, 0, tiled=True)]
    all_to_all x1, waiting for transfers between devices: 3.78 us -> 0.45 us  [body(): gathered = lax.all_to_all(spread, 'dp', 0, 0, tiled=True)]
    all_to_all x1, waiting for transfers between devices: 3.73 us -> 1.4 us  [body(): parts = lax.all_to_all(packed, 'dp', 0, 0, tiled=True)]
  transfers between devices with their start and end apart: 5 -> 7, of which waited for: 2 -> 3; matrix products, arithmetic and copies ran while one was open for 0% -> 0% of each run, Pallas kernels for 12% -> 10%
where the time goes in v5:
time: 84.9 us; the launch traced here: 83.8 us
  starting transfers between devices  40.3 us (47%)
  blocking collectives  24.4 us (29%)
  Pallas kernels  11.5 us (14%)
  waiting for transfers between devices  5.97 us (7%)
  local copies, waits for them, and re-layouts  0.95 us (1%)
    all_to_all x1, blocking collectives, body(): lax.all_to_all(joined.reshape(n_tensor, 8, SET_WIDTH + PAIR_WIDTH), 'tens...  20.4 us
    ppermute x4, starting transfers between devices, swap(): lax.ppermute(array, 'tensor', [(index, index ^ bits) for index in range(n...  12 us
    all_to_all x1, starting transfers between devices, body(): parts = lax.all_to_all(packed, 'dp', 0, 0, tiled=True)  10.2 us
    all_to_all x1, starting transfers between devices, body(): lax.all_to_all(low_spread, 'tensor', 0, 0, tiled=True, axis_index_groups=...  10.1 us
    all_to_all x1, starting transfers between devices, body(): gathered = lax.all_to_all(spread, 'dp', 0, 0, tiled=True)  7.96 us
    pallas_call x1, Pallas kernels, body(): pl.pallas_call(base_kernel, in_specs=[pl.BlockSpec(memory_space=pl.ANY),...  5.25 us
    all_to_all x1, waiting for transfers between devices, body(): lax.all_to_all(low_spread, 'tensor', 0, 0, tiled=True, axis_index_groups=...  4.11 us
    all_gather x1, blocking collectives, body(): factors = lax.all_gather(gathered, 'tensor', axis_index_groups=pairs)  3.98 us
  transfers between devices with their start and end apart: 7, of which 3 were waited for; matrix products, arithmetic and copies ran while one was open for 0% of the time, Pallas kernels for 10%

profile of v5, /device:TPU:1, one launch (start us, length us, event | category | flops | bytes accessed | tf_op | source)
XLA Modules:
  0.0 83.8 jit_solution(16662332402733558887)
XLA Ops:
  0.6 0.0 copy-start.1
  0.6 0.0 copy-start.2
  0.7 0.0 copy-start.3
  0.7 0.0 copy-start.4
  0.7 1.8 %shard_map.121.after = bf16[16,48,128]{2,1,0:T(8,128)(2,1)} custom-call(f32[1,512,128]{2,1,0:T(8,128)} %grad_a.1, f32[1,32,384]{2,1,0:T(8,128)} %bitcast.9), custom_call_target="tpu_custom_call" | custom-call | tf_op jit(solution)/shard_map/pallas_call | solution.py:173
  2.5 10.2 %all-to-all-start = ((bf16[16,48,128]{2,1,0:T(8,128)(2,1)}), bf16[16,48,128]{2,1,0:T(8,128)(2,1)S(1)}, u32[]{:S(2)}, u32[]{:S(2)}) async-start(bf16[16,48,128]{2,1,0:T(8,128)(2,1)} %shard_map.121.after), calls=%async_computation | async-start | bytes 393216 | tf_op jit(solution)/shard_map/all_to_all | solution.py:177
  12.7 5.2 %shard_map.122 = (bf16[4,256,512]{2,1,0:T(8,128)(2,1)}, bf16[4,256,512]{2,1,0:T(8,128)(2,1)}, bf16[384,256]{1,0:T(8,128)(2,1)}, f32[8,256]{1,0:T(8,128)}) custom-call(bf16[16,48,128]{2,1,0:T(8,128)(2,1)} %shard_map.121.after, s32[8,256]{1,0:T(8,128)} %bitcast.10, f32[8,256]{1,0:T(8,128)} %bitcast.11, bf16[192,384]{1,0:T(8,128)(2,1)} %hidden.1, ...), custom_call_target="tpu_custom_call" | custom-call | flops 805306368 | bytes 7340032 | tf_op jit(solution)/shard_map/pallas_call | solution.py:178
  18.0 0.0 copy-start
  18.0 0.0 copy-start.6
  18.0 3.0 %collective-permute-start = (bf16[4,256,512]{2,1,0:T(8,128)(2,1)}, bf16[4,256,512]{2,1,0:T(8,128)(2,1)S(1)}, u32[]{:S(2)}, u32[]{:S(2)}) collective-permute-start(bf16[4,256,512]{2,1,0:T(8,128)(2,1)} %get-tuple-element.22), channel_id=1, source_target_pairs={{0,1},{1,0},{2,3},{3,2},{4,5},{5,4},{6,7},{7,6},{8,9},{9,8},{10,11... | collective-permute-start | bytes 3145736 | tf_op jit(solution)/shard_map/ppermute | solution.py:163
  21.0 1.4 %all-to-all-done.parts = bf16[16,48,128]{2,1,0:T(8,128)(2,1)S(1)} async-done(((bf16[16,48,128]{2,1,0:T(8,128)(2,1)}), bf16[16,48,128]{2,1,0:T(8,128)(2,1)S(1)}, u32[]{:S(2)}, u32[]{:S(2)}) %all-to-all-start) | async-done | bytes 196640 | tf_op jit(solution)/shard_map/all_to_all | solution.py:177
  22.4 0.0 copy-done.1
  22.4 0.0 copy-done.2
  22.4 0.0 copy-done.3
  22.4 0.0 copy-done.4
  22.4 0.8 %shard_map.124 = (f32[32,128]{1,0:T(8,128)S(1)}, f32[24,32]{1,0:T(8,128)S(1)}, bf16[16,48,128]{2,1,0:T(8,128)(2,1)}) custom-call(bf16[16,48,128]{2,1,0:T(8,128)(2,1)S(1)} %all-to-all-done.parts, f32[32,128]{1,0:T(8,128)S(1)} %copy-done.1, f32[32,128]{1,0:T(8,128)S(1)} %copy-done.2, f32[24,32]{1,0:T(8,128)S(1)} %copy-done.3, f32[24,32]{1,0:T(8,128)S(1)} %copy-done.4), custom_call_target="tpu_custom_call" | custom-call | flops 17179869184 | bytes 262144 | tf_op jit(solution)/shard_map/pallas_call | solution.py:191
  23.2 8.0 %all-to-all-start.1 = ((bf16[16,48,128]{2,1,0:T(8,128)(2,1)}), bf16[16,48,128]{2,1,0:T(8,128)(2,1)S(1)}, u32[]{:S(2)}, u32[]{:S(2)}) async-start(bf16[16,48,128]{2,1,0:T(8,128)(2,1)} %get-tuple-element.24), calls=%async_computation.1 | async-start | bytes 393216 | tf_op jit(solution)/shard_map/all_to_all | solution.py:201
  31.2 0.0 collective-permute-done.other
  31.2 0.0 copy-done
  31.2 0.9 %shard_map.123 = (bf16[256,512]{1,0:T(8,128)(2,1)}, bf16[256,512]{1,0:T(8,128)(2,1)S(1)}, bf16[256,512]{1,0:T(8,128)(2,1)S(1)}, f32[256,512]{1,0:T(8,128)S(1)}) custom-call(bf16[4,256,512]{2,1,0:T(8,128)(2,1)S(1)} %copy-done, bf16[4,256,512]{2,1,0:T(8,128)(2,1)S(1)} %collective-permute-done.other), custom_call_target="tpu_custom_call" | custom-call | flops 1048576 | bytes 4194304 | tf_op jit(solution)/shard_map/pallas_call | solution.py:203
  32.1 2.3 %collective-permute-start.1 = (bf16[256,512]{1,0:T(8,128)(2,1)}, bf16[256,512]{1,0:T(8,128)(2,1)S(1)}, u32[]{:S(2)}, u32[]{:S(2)}) collective-permute-start(bf16[256,512]{1,0:T(8,128)(2,1)} %get-tuple-element.36), channel_id=1, source_target_pairs={{0,2},{1,3},{2,0},{3,1},{4,6},{5,7},{6,4},{7,5},{8,10},{9,11},{10,... | collective-permute-start | bytes 786440 | tf_op jit(solution)/shard_map/ppermute | solution.py:163
  34.4 4.0 %collective-permute-start.2 = (bf16[256,512]{1,0:T(8,128)(2,1)S(1)}, bf16[256,512]{1,0:T(8,128)(2,1)S(1)}, u32[]{:S(2)}, u32[]{:S(2)}) collective-permute-start(bf16[256,512]{1,0:T(8,128)(2,1)S(1)} %get-tuple-element.37), channel_id=1, source_target_pairs={{0,4},{1,5},{2,6},{3,7},{4,0},{5,1},{6,2},{7,3},{8,12},{9,13},{10,... | collective-permute-start | bytes 786440 | tf_op jit(solution)/shard_map/ppermute | solution.py:163
  38.4 2.7 %collective-permute-start.3 = (bf16[256,512]{1,0:T(8,128)(2,1)S(1)}, bf16[256,512]{1,0:T(8,128)(2,1)S(1)}, u32[]{:S(2)}, u32[]{:S(2)}) collective-permute-start(bf16[256,512]{1,0:T(8,128)(2,1)S(1)} %get-tuple-element.38), channel_id=1, source_target_pairs={{0,6},{1,7},{2,4},{3,5},{4,2},{5,3},{6,0},{7,1},{8,14},{9,15},{10,... | collective-permute-start | bytes 786440 | tf_op jit(solution)/shard_map/ppermute | solution.py:163
  41.1 0.4 all-to-all-done.1.gathered
  41.6 0.0 copy-done.6
  41.6 0.0 copy-start.5
  41.6 0.9 %copy-done.5 = bf16[384,256]{1,0:T(8,128)(2,1)S(1)} copy-done((bf16[384,256]{1,0:T(8,128)(2,1)S(1)}, bf16[384,256]{1,0:T(8,128)(2,1)}, u32[]{:S(2)}) %copy-start.5) | copy-done | bytes 196632
  42.5 1.0 %shard_map.125 = bf16[16,32,256]{2,1,0:T(8,128)(2,1)} custom-call(bf16[16,48,128]{2,1,0:T(8,128)(2,1)S(1)} %all-to-all-done.1.gathered, bf16[384,256]{1,0:T(8,128)(2,1)S(1)} %copy-done.5, f32[8,256]{1,0:T(8,128)S(1)} %copy-done.6), custom_call_target="tpu_custom_call" | custom-call | flops 17179869184 | bytes 262144 | tf_op jit(solution)/shard_map/pallas_call | solution.py:210
  43.5 10.1 %all-to-all-start.2 = ((bf16[16,32,256]{2,1,0:T(8,128)(2,1)}), bf16[16,32,256]{2,1,0:T(8,128)(2,1)S(1)}, u32[]{:S(2)}, u32[]{:S(2)}) async-start(bf16[16,32,256]{2,1,0:T(8,128)(2,1)} %shard_map.125), calls=%async_computation.2 | async-start | bytes 524288 | tf_op jit(solution)/shard_map/all_to_all | solution.py:223
  53.6 0.6 shard_map.126
  54.2 4.0 %all-gather = bf16[32,48,128]{2,1,0:T(8,128)(2,1)S(1)} all-gather(bf16[16,48,128]{2,1,0:T(8,128)(2,1)S(1)} %all-to-all-done.1.gathered), channel_id=2, replica_groups={{0,1},{2,3},{4,5},{6,7},{8,9},{10,11},{12,13},{14,15},{16,17},{18,19},{..., dimensions={0}, use_global_device_ids=true | all-gather | bytes 589824 | tf_op jit(solution)/shard_map/all_gather | solution.py:224
  58.2 0.0 collective-permute-done.1.other_1
  58.2 0.0 collective-permute-done.2.other_2
  58.2 0.0 collective-permute-done.3.other_3
  58.2 0.1 shard_map.127.base
  58.4 4.1 %all-to-all-done.2 = bf16[16,32,256]{2,1,0:T(8,128)(2,1)S(1)} async-done(((bf16[16,32,256]{2,1,0:T(8,128)(2,1)}), bf16[16,32,256]{2,1,0:T(8,128)(2,1)S(1)}, u32[]{:S(2)}, u32[]{:S(2)}) %all-to-all-start.2) | async-done | bytes 262176 | tf_op jit(solution)/shard_map/all_to_all | solution.py:223
  62.5 0.3 shard_map.128
  62.8 20.4 %all_to_all.20.parts = bf16[32,8,768]{2,1,0:T(8,128)(2,1)S(1)} all-to-all(bf16[32,8,768]{2,1,0:T(8,128)(2,1)S(1)} %bitcast.7), channel_id=1, replica_groups=mesh['dp'=16,'tensor'=32] {'tensor'}, dimensions={0} | all-to-all | bytes 786432 | tf_op jit(solution)/shard_map/all_to_all | solution.py:237
  83.2 0.7 shard_map.129
Async XLA Ops:
  0.6 21.7 %copy-start.1 = (f32[32,128]{1,0:T(8,128)S(1)}, f32[32,128]{1,0:T(8,128)}, u32[]{:S(2)}) copy-start(f32[32,128]{1,0:T(8,128)} %factor_a.3) | copy-start | bytes 49156
  0.6 21.7 %copy-start.2 = (f32[32,128]{1,0:T(8,128)S(1)}, f32[32,128]{1,0:T(8,128)}, u32[]{:S(2)}) copy-start(f32[32,128]{1,0:T(8,128)} %moment_a.3) | copy-start | bytes 49156
  0.7 21.7 %copy-start.3 = (f32[24,32]{1,0:T(8,128)S(1)}, f32[24,32]{1,0:T(8,128)}, u32[]{:S(2)}) copy-start(f32[24,32]{1,0:T(8,128)} %factor_b.3) | copy-start | bytes 9220
  0.7 21.7 %copy-start.4 = (f32[24,32]{1,0:T(8,128)S(1)}, f32[24,32]{1,0:T(8,128)}, u32[]{:S(2)}) copy-start(f32[24,32]{1,0:T(8,128)} %moment_b.3) | copy-start | bytes 9220
  2.5 19.9 %all-to-all-start = ((bf16[16,48,128]{2,1,0:T(8,128)(2,1)}), bf16[16,48,128]{2,1,0:T(8,128)(2,1)S(1)}, u32[]{:S(2)}, u32[]{:S(2)}) async-start(bf16[16,48,128]{2,1,0:T(8,128)(2,1)} %shard_map.121.after), calls=%async_computation | async-start | bytes 393216 | tf_op jit(solution)/shard_map/all_to_all | solution.py:177
  18.0 13.2 %copy-start = (bf16[4,256,512]{2,1,0:T(8,128)(2,1)S(1)}, bf16[4,256,512]{2,1,0:T(8,128)(2,1)}, u32[]{:S(2)}) copy-start(bf16[4,256,512]{2,1,0:T(8,128)(2,1)} %get-tuple-element.21.own) | copy-start | bytes 3145732
  18.0 23.6 %copy-start.6 = (f32[8,256]{1,0:T(8,128)S(1)}, f32[8,256]{1,0:T(8,128)}, u32[]{:S(2)}) copy-start(f32[8,256]{1,0:T(8,128)} %get-tuple-element.26.row_weights) | copy-start | bytes 24580
  18.0 13.2 %collective-permute-start = (bf16[4,256,512]{2,1,0:T(8,128)(2,1)}, bf16[4,256,512]{2,1,0:T(8,128)(2,1)S(1)}, u32[]{:S(2)}, u32[]{:S(2)}) collective-permute-start(bf16[4,256,512]{2,1,0:T(8,128)(2,1)} %get-tuple-element.22), channel_id=1, source_target_pairs={{0,1},{1,0},{2,3},{3,2},{4,5},{5,4},{6,7},{7,6},{8,9},{9,8},{10,11... | collective-permute-start | bytes 3145736 | tf_op jit(solution)/shard_map/ppermute | solution.py:163
  23.2 18.3 %all-to-all-start.1 = ((bf16[16,48,128]{2,1,0:T(8,128)(2,1)}), bf16[16,48,128]{2,1,0:T(8,128)(2,1)S(1)}, u32[]{:S(2)}, u32[]{:S(2)}) async-start(bf16[16,48,128]{2,1,0:T(8,128)(2,1)} %get-tuple-element.24), calls=%async_computation.1 | async-start | bytes 393216 | tf_op jit(solution)/shard_map/all_to_all | solution.py:201
  32.1 26.1 %collective-permute-start.1 = (bf16[256,512]{1,0:T(8,128)(2,1)}, bf16[256,512]{1,0:T(8,128)(2,1)S(1)}, u32[]{:S(2)}, u32[]{:S(2)}) collective-permute-start(bf16[256,512]{1,0:T(8,128)(2,1)} %get-tuple-element.36), channel_id=1, source_target_pairs={{0,2},{1,3},{2,0},{3,1},{4,6},{5,7},{6,4},{7,5},{8,10},{9,11},{10,... | collective-permute-start | bytes 786440 | tf_op jit(solution)/shard_map/ppermute | solution.py:163
  34.4 23.8 %collective-permute-start.2 = (bf16[256,512]{1,0:T(8,128)(2,1)S(1)}, bf16[256,512]{1,0:T(8,128)(2,1)S(1)}, u32[]{:S(2)}, u32[]{:S(2)}) collective-permute-start(bf16[256,512]{1,0:T(8,128)(2,1)S(1)} %get-tuple-element.37), channel_id=1, source_target_pairs={{0,4},{1,5},{2,6},{3,7},{4,0},{5,1},{6,2},{7,3},{8,12},{9,13},{10,... | collective-permute-start | bytes 786440 | tf_op jit(solution)/shard_map/ppermute | solution.py:163
  38.4 19.8 %collective-permute-start.3 = (bf16[256,512]{1,0:T(8,128)(2,1)S(1)}, bf16[256,512]{1,0:T(8,128)(2,1)S(1)}, u32[]{:S(2)}, u32[]{:S(2)}) collective-permute-start(bf16[256,512]{1,0:T(8,128)(2,1)S(1)} %get-tuple-element.38), channel_id=1, source_target_pairs={{0,6},{1,7},{2,4},{3,5},{4,2},{5,3},{6,0},{7,1},{8,14},{9,15},{10,... | collective-permute-start | bytes 786440 | tf_op jit(solution)/shard_map/ppermute | solution.py:163
  41.6 0.9 %copy-start.5 = (bf16[384,256]{1,0:T(8,128)(2,1)S(1)}, bf16[384,256]{1,0:T(8,128)(2,1)}, u32[]{:S(2)}) copy-start(bf16[384,256]{1,0:T(8,128)(2,1)} %get-tuple-element.25.rows_t) | copy-start | bytes 589828
  43.5 19.0 %all-to-all-start.2 = ((bf16[16,32,256]{2,1,0:T(8,128)(2,1)}), bf16[16,32,256]{2,1,0:T(8,128)(2,1)S(1)}, u32[]{:S(2)}, u32[]{:S(2)}) async-start(bf16[16,32,256]{2,1,0:T(8,128)(2,1)} %shard_map.125), calls=%async_computation.2 | async-start | bytes 524288 | tf_op jit(solution)/shard_map/all_to_all | solution.py:223

commit v6 on v5

--- a/solution.py
+++ b/solution.py
@@ -62,29 +62,33 @@
 def base_kernel(after, ids, weights, hidden, base, send, own, rows_t, row_weights, rows, column):
     index = lax.axis_index("tensor")
     expert, core = index // 2, index % 2
-    named = ids[...] == expert
-    hit = jnp.sum(jnp.where(named, 1.0, 0.0), axis=0, keepdims=True)
-    weight = jnp.sum(jnp.where(named, weights[...], 0.0), axis=0, keepdims=True)
-    one = lax.broadcasted_iota(jnp.int32, (TOKENS, TOKENS), 0)
-    two = lax.broadcasted_iota(jnp.int32, (TOKENS, TOKENS), 1)
-    earlier = jnp.where(one < two, 1.0, 0.0).astype(BF16)
-    wide = jnp.broadcast_to(hit, (8, TOKENS)).astype(BF16)
-    before = jnp.dot(wide, earlier, preferred_element_type=F32)[0:1]
-    slot = jnp.where(hit > 0.5, before, -1.0)
-    both = jnp.concatenate([slot, weight, jnp.zeros((6, TOKENS), F32)], axis=0).T
-    slots = lax.broadcasted_iota(jnp.int32, (TOKENS, SLOTS), 1)
-    chosen = jnp.where(both[:, 0:1].astype(jnp.int32) == slots, 1.0, 0.0).astype(BF16)
-    rows[...] = jnp.dot(chosen, hidden[...], preferred_element_type=F32).astype(BF16)
-    column[...] = jnp.broadcast_to(both[:, 1:2], (TOKENS, 128))
-    slots_t = lax.broadcasted_iota(jnp.int32, (SLOTS, TOKENS), 0)
-    chosen_t = jnp.where(slot.astype(jnp.int32) == slots_t, 1.0, 0.0).astype(BF16)
-    rows_t[...] = first_rows(hidden[...], chosen_t).astype(BF16)
-    row_weights[...] = jnp.broadcast_to(weight, (8, TOKENS))
+
+    @pl.when(pl.program_id(0) == 0)
+    def _():
+        named = ids[...] == expert
+        hit = jnp.sum(jnp.where(named, 1.0, 0.0), axis=0, keepdims=True)
+        weight = jnp.sum(jnp.where(named, weights[...], 0.0), axis=0, keepdims=True)
+        one = lax.broadcasted_iota(jnp.int32, (TOKENS, TOKENS), 0)
+        two = lax.broadcasted_iota(jnp.int32, (TOKENS, TOKENS), 1)
+        earlier = jnp.where(one < two, 1.0, 0.0).astype(BF16)
+        wide = jnp.broadcast_to(hit, (8, TOKENS)).astype(BF16)
+        before = jnp.dot(wide, earlier, preferred_element_type=F32)[0:1]
+        slot = jnp.where(hit > 0.5, before, -1.0)
+        both = jnp.concatenate([slot, weight, jnp.zeros((6, TOKENS), F32)], axis=0).T
+        slots = lax.broadcasted_iota(jnp.int32, (TOKENS, SLOTS), 1)
+        chosen = jnp.where(both[:, 0:1].astype(jnp.int32) == slots, 1.0, 0.0).astype(BF16)
+        rows[...] = jnp.dot(chosen, hidden[...], preferred_element_type=F32).astype(BF16)
+        column[...] = jnp.broadcast_to(both[:, 1:2], (TOKENS, 128))
+        slots_t = lax.broadcasted_iota(jnp.int32, (SLOTS, TOKENS), 0)
+        chosen_t = jnp.where(slot.astype(jnp.int32) == slots_t, 1.0, 0.0).astype(BF16)
+        rows_t[...] = first_rows(hidden[...], chosen_t).astype(BF16)
+        row_weights[...] = jnp.broadcast_to(weight, (8, TOKENS))
+
     for mine in range(2):
 
         @pl.when(core == mine)
         def _(mine=mine):
-            for place in range(4):
+            for place in range(2):
                 for side, out in ((1 - mine, send), (mine, own)):
                     at = (2 * place + side) * SET_WIDTH
                     part = jnp.dot(rows[...], base[:, at : at + SET_WIDTH], preferred_element_type=F32)
@@ -97,7 +101,7 @@
     low = place % 2
     flipped = (place + 1 - 2 * low, (place + 2) % 4, 3 - place)
     for there, send in zip(flipped, (send_1, send_2, send_3)):
-        send[...] = (own[there].astype(F32) + other[there].astype(F32)).astype(BF16)
+        send[...] = own[there] + other[there]
 
 
 def low_rank_kernel(gathered, rows_t, row_weights, spread, b_scr):
@@ -162,7 +166,10 @@
     def swap(array, bits):
         return lax.ppermute(array, "tensor", [(index, index ^ bits) for index in range(n_tensor)])
 
-    vmem = pl.BlockSpec(memory_space=pltpu.VMEM)
+    half = pl.BlockSpec((2, TOKENS, SET_WIDTH), lambda step: (step, 0, 0))
+
+    def whole(dims):
+        return pl.BlockSpec(dims, lambda step: (0,) * len(dims))
 
     def limit(size):
         return pltpu.CompilerParams(vmem_limit_bytes=size * 2**20)
@@ -177,7 +184,15 @@
     parts = lax.all_to_all(packed, "dp", 0, 0, tiled=True)
     send, own, rows_t, row_weights = pl.pallas_call(
         base_kernel,
-        in_specs=[pl.BlockSpec(memory_space=pl.ANY), vmem, vmem, vmem, vmem],
+        grid=(2,),
+        in_specs=[
+            pl.BlockSpec(memory_space=pl.ANY),
+            whole((8, TOKENS)),
+            whole((8, TOKENS)),
+            whole((SLOTS, HIDDEN)),
+            pl.BlockSpec((HIDDEN, WIDTH // 2), lambda step: (0, step)),
+        ],
+        out_specs=[half, half, whole((HIDDEN, TOKENS)), whole((8, TOKENS))],
         out_shape=(
             shape((4, TOKENS, SET_WIDTH), BF16),
             shape((4, TOKENS, SET_WIDTH), BF16),

time: 84.9 us -> 84.3 us (level)
  no operation moved by 1% of the time
where the time goes in v6:
time: 84.3 us; the launch traced here: 83.2 us
  starting transfers between devices  39.7 us (47%)
  blocking collectives  24.5 us (29%)
  Pallas kernels  10.8 us (13%)
  waiting for transfers between devices  6.52 us (8%)
  local copies, waits for them, and re-layouts  0.95 us (1%)
    all_to_all x1, blocking collectives, body(): lax.all_to_all(joined.reshape(n_tensor, 8, SET_WIDTH + PAIR_WIDTH), 'tens...  20.5 us
    ppermute x4, starting transfers between devices, swap(): lax.ppermute(array, 'tensor', [(index, index ^ bits) for index in range(n...  12 us
    all_to_all x1, starting transfers between devices, body(): parts = lax.all_to_all(packed, 'dp', 0, 0, tiled=True)  10.2 us
    all_to_all x1, starting transfers between devices, body(): lax.all_to_all(low_spread, 'tensor', 0, 0, tiled=True, axis_index_groups=...  10.1 us
    all_to_all x1, starting transfers between devices, body(): gathered = lax.all_to_all(spread, 'dp', 0, 0, tiled=True)  7.34 us
    pallas_call x1, Pallas kernels, body(): pl.pallas_call(base_kernel, grid=(2,), in_specs=[pl.BlockSpec(memory_spac...  4.58 us
    all_to_all x1, waiting for transfers between devices, body(): lax.all_to_all(low_spread, 'tensor', 0, 0, tiled=True, axis_index_groups=...  3.99 us
    all_gather x1, blocking collectives, body(): factors = lax.all_gather(gathered, 'tensor', axis_index_groups=pairs)  3.97 us
  transfers between devices with their start and end apart: 7, of which 3 were waited for; matrix products, arithmetic and copies ran while one was open for 0% of the time, Pallas kernels for 10%

profile of v6, /device:TPU:1, one launch (start us, length us, event | category | flops | bytes accessed | tf_op | source)
XLA Modules:
  0.0 83.2 jit_solution(3378853883111712363)
XLA Ops:
  0.6 0.0 copy-start.1
  0.6 0.0 copy-start.2
  0.7 0.0 copy-start.3
  0.7 0.0 copy-start.4
  0.7 1.8 %shard_map.121.after = bf16[16,48,128]{2,1,0:T(8,128)(2,1)} custom-call(f32[1,512,128]{2,1,0:T(8,128)} %grad_a.1, f32[1,32,384]{2,1,0:T(8,128)} %bitcast.9), custom_call_target="tpu_custom_call" | custom-call | tf_op jit(solution)/shard_map/pallas_call | solution.py:180
  2.5 10.2 %all-to-all-start = ((bf16[16,48,128]{2,1,0:T(8,128)(2,1)}), bf16[16,48,128]{2,1,0:T(8,128)(2,1)S(1)}, u32[]{:S(2)}, u32[]{:S(2)}) async-start(bf16[16,48,128]{2,1,0:T(8,128)(2,1)} %shard_map.121.after), calls=%async_computation | async-start | bytes 393216 | tf_op jit(solution)/shard_map/all_to_all | solution.py:184
  12.7 4.6 %shard_map.122 = (bf16[4,256,512]{2,1,0:T(8,128)(2,1)}, bf16[4,256,512]{2,1,0:T(8,128)(2,1)}, bf16[384,256]{1,0:T(8,128)(2,1)}, f32[8,256]{1,0:T(8,128)}) custom-call(bf16[16,48,128]{2,1,0:T(8,128)(2,1)} %shard_map.121.after, s32[8,256]{1,0:T(8,128)} %bitcast.10, f32[8,256]{1,0:T(8,128)} %bitcast.11, bf16[192,384]{1,0:T(8,128)(2,1)} %hidden.1, ...), custom_call_target="tpu_custom_call" | custom-call | flops 805306368 | bytes 7340032 | tf_op jit(solution)/shard_map/pallas_call | solution.py:185
  17.3 0.0 copy-start
  17.3 0.0 copy-start.6
  17.3 3.0 %collective-permute-start = (bf16[4,256,512]{2,1,0:T(8,128)(2,1)}, bf16[4,256,512]{2,1,0:T(8,128)(2,1)S(1)}, u32[]{:S(2)}, u32[]{:S(2)}) collective-permute-start(bf16[4,256,512]{2,1,0:T(8,128)(2,1)} %get-tuple-element.22), channel_id=1, source_target_pairs={{0,1},{1,0},{2,3},{3,2},{4,5},{5,4},{6,7},{7,6},{8,9},{9,8},{10,11... | collective-permute-start | bytes 3145736 | tf_op jit(solution)/shard_map/ppermute | solution.py:167
  20.3 2.0 %all-to-all-done.parts = bf16[16,48,128]{2,1,0:T(8,128)(2,1)S(1)} async-done(((bf16[16,48,128]{2,1,0:T(8,128)(2,1)}), bf16[16,48,128]{2,1,0:T(8,128)(2,1)S(1)}, u32[]{:S(2)}, u32[]{:S(2)}) %all-to-all-start) | async-done | bytes 196640 | tf_op jit(solution)/shard_map/all_to_all | solution.py:184
  22.4 0.0 copy-done.1
  22.4 0.0 copy-done.2
  22.4 0.0 copy-done.3
  22.4 0.0 copy-done.4
  22.4 0.8 %shard_map.124 = (f32[32,128]{1,0:T(8,128)S(1)}, f32[24,32]{1,0:T(8,128)S(1)}, bf16[16,48,128]{2,1,0:T(8,128)(2,1)}) custom-call(bf16[16,48,128]{2,1,0:T(8,128)(2,1)S(1)} %all-to-all-done.parts, f32[32,128]{1,0:T(8,128)S(1)} %copy-done.1, f32[32,128]{1,0:T(8,128)S(1)} %copy-done.2, f32[24,32]{1,0:T(8,128)S(1)} %copy-done.3, f32[24,32]{1,0:T(8,128)S(1)} %copy-done.4), custom_call_target="tpu_custom_call" | custom-call | flops 17179869184 | bytes 262144 | tf_op jit(solution)/shard_map/pallas_call | solution.py:206
  23.2 7.3 %all-to-all-start.1 = ((bf16[16,48,128]{2,1,0:T(8,128)(2,1)}), bf16[16,48,128]{2,1,0:T(8,128)(2,1)S(1)}, u32[]{:S(2)}, u32[]{:S(2)}) async-start(bf16[16,48,128]{2,1,0:T(8,128)(2,1)} %get-tuple-element.24), calls=%async_computation.1 | async-start | bytes 393216 | tf_op jit(solution)/shard_map/all_to_all | solution.py:216
  30.6 0.0 collective-permute-done.other
  30.6 0.0 copy-done
  30.6 0.8 %shard_map.123 = (bf16[256,512]{1,0:T(8,128)(2,1)}, bf16[256,512]{1,0:T(8,128)(2,1)S(1)}, bf16[256,512]{1,0:T(8,128)(2,1)S(1)}, f32[256,512]{1,0:T(8,128)S(1)}) custom-call(bf16[4,256,512]{2,1,0:T(8,128)(2,1)S(1)} %copy-done, bf16[4,256,512]{2,1,0:T(8,128)(2,1)S(1)} %collective-permute-done.other), custom_call_target="tpu_custom_call" | custom-call | flops 1048576 | bytes 4194304 | tf_op jit(solution)/shard_map/pallas_call | solution.py:218
  31.4 2.3 %collective-permute-start.1 = (bf16[256,512]{1,0:T(8,128)(2,1)}, bf16[256,512]{1,0:T(8,128)(2,1)S(1)}, u32[]{:S(2)}, u32[]{:S(2)}) collective-permute-start(bf16[256,512]{1,0:T(8,128)(2,1)} %get-tuple-element.36), channel_id=1, source_target_pairs={{0,2},{1,3},{2,0},{3,1},{4,6},{5,7},{6,4},{7,5},{8,10},{9,11},{10,... | collective-permute-start | bytes 786440 | tf_op jit(solution)/shard_map/ppermute | solution.py:167
  33.7 4.0 %collective-permute-start.2 = (bf16[256,512]{1,0:T(8,128)(2,1)S(1)}, bf16[256,512]{1,0:T(8,128)(2,1)S(1)}, u32[]{:S(2)}, u32[]{:S(2)}) collective-permute-start(bf16[256,512]{1,0:T(8,128)(2,1)S(1)} %get-tuple-element.37), channel_id=1, source_target_pairs={{0,4},{1,5},{2,6},{3,7},{4,0},{5,1},{6,2},{7,3},{8,12},{9,13},{10,... | collective-permute-start | bytes 786440 | tf_op jit(solution)/shard_map/ppermute | solution.py:167
  37.7 2.7 %collective-permute-start.3 = (bf16[256,512]{1,0:T(8,128)(2,1)S(1)}, bf16[256,512]{1,0:T(8,128)(2,1)S(1)}, u32[]{:S(2)}, u32[]{:S(2)}) collective-permute-start(bf16[256,512]{1,0:T(8,128)(2,1)S(1)} %get-tuple-element.38), channel_id=1, source_target_pairs={{0,6},{1,7},{2,4},{3,5},{4,2},{5,3},{6,0},{7,1},{8,14},{9,15},{10,... | collective-permute-start | bytes 786440 | tf_op jit(solution)/shard_map/ppermute | solution.py:167
  40.4 0.5 all-to-all-done.1.gathered
  40.9 0.0 copy-done.6
  40.9 0.0 copy-start.5
  40.9 0.9 %copy-done.5 = bf16[384,256]{1,0:T(8,128)(2,1)S(1)} copy-done((bf16[384,256]{1,0:T(8,128)(2,1)S(1)}, bf16[384,256]{1,0:T(8,128)(2,1)}, u32[]{:S(2)}) %copy-start.5) | copy-done | bytes 196632
  41.9 1.0 %shard_map.125 = bf16[16,32,256]{2,1,0:T(8,128)(2,1)} custom-call(bf16[16,48,128]{2,1,0:T(8,128)(2,1)S(1)} %all-to-all-done.1.gathered, bf16[384,256]{1,0:T(8,128)(2,1)S(1)} %copy-done.5, f32[8,256]{1,0:T(8,128)S(1)} %copy-done.6), custom_call_target="tpu_custom_call" | custom-call | flops 17179869184 | bytes 262144 | tf_op jit(solution)/shard_map/pallas_call | solution.py:225
  42.9 10.1 %all-to-all-start.2 = ((bf16[16,32,256]{2,1,0:T(8,128)(2,1)}), bf16[16,32,256]{2,1,0:T(8,128)(2,1)S(1)}, u32[]{:S(2)}, u32[]{:S(2)}) async-start(bf16[16,32,256]{2,1,0:T(8,128)(2,1)} %shard_map.125), calls=%async_computation.2 | async-start | bytes 524288 | tf_op jit(solution)/shard_map/all_to_all | solution.py:238
  53.0 0.6 shard_map.126
  53.6 4.0 %all-gather = bf16[32,48,128]{2,1,0:T(8,128)(2,1)S(1)} all-gather(bf16[16,48,128]{2,1,0:T(8,128)(2,1)S(1)} %all-to-all-done.1.gathered), channel_id=2, replica_groups={{0,1},{2,3},{4,5},{6,7},{8,9},{10,11},{12,13},{14,15},{16,17},{18,19},{..., dimensions={0}, use_global_device_ids=true | all-gather | bytes 589824 | tf_op jit(solution)/shard_map/all_gather | solution.py:239
  57.6 0.0 collective-permute-done.1.other_1
  57.6 0.0 collective-permute-done.2.other_2
  57.6 0.0 collective-permute-done.3.other_3
  57.6 0.1 shard_map.127.base
  57.7 4.0 %all-to-all-done.2 = bf16[16,32,256]{2,1,0:T(8,128)(2,1)S(1)} async-done(((bf16[16,32,256]{2,1,0:T(8,128)(2,1)}), bf16[16,32,256]{2,1,0:T(8,128)(2,1)S(1)}, u32[]{:S(2)}, u32[]{:S(2)}) %all-to-all-start.2) | async-done | bytes 262176 | tf_op jit(solution)/shard_map/all_to_all | solution.py:238
  61.7 0.3 shard_map.128
  62.0 20.5 %all_to_all.20.parts = bf16[32,8,768]{2,1,0:T(8,128)(2,1)S(1)} all-to-all(bf16[32,8,768]{2,1,0:T(8,128)(2,1)S(1)} %bitcast.7), channel_id=1, replica_groups=mesh['dp'=16,'tensor'=32] {'tensor'}, dimensions={0} | all-to-all | bytes 786432 | tf_op jit(solution)/shard_map/all_to_all | solution.py:252
  82.5 0.7 shard_map.129
Async XLA Ops:
  0.6 21.7 %copy-start.1 = (f32[32,128]{1,0:T(8,128)S(1)}, f32[32,128]{1,0:T(8,128)}, u32[]{:S(2)}) copy-start(f32[32,128]{1,0:T(8,128)} %factor_a.3) | copy-start | bytes 49156
  0.6 21.7 %copy-start.2 = (f32[32,128]{1,0:T(8,128)S(1)}, f32[32,128]{1,0:T(8,128)}, u32[]{:S(2)}) copy-start(f32[32,128]{1,0:T(8,128)} %moment_a.3) | copy-start | bytes 49156
  0.7 21.7 %copy-start.3 = (f32[24,32]{1,0:T(8,128)S(1)}, f32[24,32]{1,0:T(8,128)}, u32[]{:S(2)}) copy-start(f32[24,32]{1,0:T(8,128)} %factor_b.3) | copy-start | bytes 9220
  0.7 21.7 %copy-start.4 = (f32[24,32]{1,0:T(8,128)S(1)}, f32[24,32]{1,0:T(8,128)}, u32[]{:S(2)}) copy-start(f32[24,32]{1,0:T(8,128)} %moment_b.3) | copy-start | bytes 9220
  2.5 19.9 %all-to-all-start = ((bf16[16,48,128]{2,1,0:T(8,128)(2,1)}), bf16[16,48,128]{2,1,0:T(8,128)(2,1)S(1)}, u32[]{:S(2)}, u32[]{:S(2)}) async-start(bf16[16,48,128]{2,1,0:T(8,128)(2,1)} %shard_map.121.after), calls=%async_computation | async-start | bytes 393216 | tf_op jit(solution)/shard_map/all_to_all | solution.py:184
  17.3 13.3 %copy-start = (bf16[4,256,512]{2,1,0:T(8,128)(2,1)S(1)}, bf16[4,256,512]{2,1,0:T(8,128)(2,1)}, u32[]{:S(2)}) copy-start(bf16[4,256,512]{2,1,0:T(8,128)(2,1)} %get-tuple-element.21.own) | copy-start | bytes 3145732
  17.3 23.6 %copy-start.6 = (f32[8,256]{1,0:T(8,128)S(1)}, f32[8,256]{1,0:T(8,128)}, u32[]{:S(2)}) copy-start(f32[8,256]{1,0:T(8,128)} %get-tuple-element.26.row_weights) | copy-start | bytes 24580
  17.3 13.3 %collective-permute-start = (bf16[4,256,512]{2,1,0:T(8,128)(2,1)}, bf16[4,256,512]{2,1,0:T(8,128)(2,1)S(1)}, u32[]{:S(2)}, u32[]{:S(2)}) collective-permute-start(bf16[4,256,512]{2,1,0:T(8,128)(2,1)} %get-tuple-element.22), channel_id=1, source_target_pairs={{0,1},{1,0},{2,3},{3,2},{4,5},{5,4},{6,7},{7,6},{8,9},{9,8},{10,11... | collective-permute-start | bytes 3145736 | tf_op jit(solution)/shard_map/ppermute | solution.py:167
  23.2 17.7 %all-to-all-start.1 = ((bf16[16,48,128]{2,1,0:T(8,128)(2,1)}), bf16[16,48,128]{2,1,0:T(8,128)(2,1)S(1)}, u32[]{:S(2)}, u32[]{:S(2)}) async-start(bf16[16,48,128]{2,1,0:T(8,128)(2,1)} %get-tuple-element.24), calls=%async_computation.1 | async-start | bytes 393216 | tf_op jit(solution)/shard_map/all_to_all | solution.py:216
  31.4 26.2 %collective-permute-start.1 = (bf16[256,512]{1,0:T(8,128)(2,1)}, bf16[256,512]{1,0:T(8,128)(2,1)S(1)}, u32[]{:S(2)}, u32[]{:S(2)}) collective-permute-start(bf16[256,512]{1,0:T(8,128)(2,1)} %get-tuple-element.36), channel_id=1, source_target_pairs={{0,2},{1,3},{2,0},{3,1},{4,6},{5,7},{6,4},{7,5},{8,10},{9,11},{10,... | collective-permute-start | bytes 786440 | tf_op jit(solution)/shard_map/ppermute | solution.py:167
  33.7 23.9 %collective-permute-start.2 = (bf16[256,512]{1,0:T(8,128)(2,1)S(1)}, bf16[256,512]{1,0:T(8,128)(2,1)S(1)}, u32[]{:S(2)}, u32[]{:S(2)}) collective-permute-start(bf16[256,512]{1,0:T(8,128)(2,1)S(1)} %get-tuple-element.37), channel_id=1, source_target_pairs={{0,4},{1,5},{2,6},{3,7},{4,0},{5,1},{6,2},{7,3},{8,12},{9,13},{10,... | collective-permute-start | bytes 786440 | tf_op jit(solution)/shard_map/ppermute | solution.py:167
  37.7 19.9 %collective-permute-start.3 = (bf16[256,512]{1,0:T(8,128)(2,1)S(1)}, bf16[256,512]{1,0:T(8,128)(2,1)S(1)}, u32[]{:S(2)}, u32[]{:S(2)}) collective-permute-start(bf16[256,512]{1,0:T(8,128)(2,1)S(1)} %get-tuple-element.38), channel_id=1, source_target_pairs={{0,6},{1,7},{2,4},{3,5},{4,2},{5,3},{6,0},{7,1},{8,14},{9,15},{10,... | collective-permute-start | bytes 786440 | tf_op jit(solution)/shard_map/ppermute | solution.py:167
  40.9 0.9 %copy-start.5 = (bf16[384,256]{1,0:T(8,128)(2,1)S(1)}, bf16[384,256]{1,0:T(8,128)(2,1)}, u32[]{:S(2)}) copy-start(bf16[384,256]{1,0:T(8,128)(2,1)} %get-tuple-element.25.rows_t) | copy-start | bytes 589828
  42.9 18.9 %all-to-all-start.2 = ((bf16[16,32,256]{2,1,0:T(8,128)(2,1)}), bf16[16,32,256]{2,1,0:T(8,128)(2,1)S(1)}, u32[]{:S(2)}, u32[]{:S(2)}) async-start(bf16[16,32,256]{2,1,0:T(8,128)(2,1)} %shard_map.125), calls=%async_computation.2 | async-start | bytes 524288 | tf_op jit(solution)/shard_map/all_to_all | solution.py:238

commit v7 on v6

--- a/solution.py
+++ b/solution.py
@@ -221,7 +221,7 @@
         compiler_params=limit(12),
         cost_estimate=cost(2**20, 4 * 2**20),
     )(own, other)
-    others = [swap(send_1, 2), swap(send_2, 4), swap(send_3, 6)]
+    others = [swap(send_3, 6), swap(send_2, 4), swap(send_1, 2)]
     low_spread = pl.pallas_call(
         low_rank_kernel,
         out_shape=shape((CHIPS, RANK, TOKENS), BF16),

time: 84.3 us -> 84 us (level)
  no operation moved by 1% of the time
where the time goes in v7:
time: 84 us; the launch traced here: 83.2 us
  starting transfers between devices  39.7 us (47%)
  blocking collectives  24.5 us (29%)
  Pallas kernels  10.8 us (13%)
  waiting for transfers between devices  6.52 us (8%)
  local copies, waits for them, and re-layouts  0.95 us (1%)
    all_to_all x1, blocking collectives, body(): lax.all_to_all(joined.reshape(n_tensor, 8, SET_WIDTH + PAIR_WIDTH), 'tens...  20.5 us
    ppermute x4, starting transfers between devices, swap(): lax.ppermute(array, 'tensor', [(index, index ^ bits) for index in range(n...  12 us
    all_to_all x1, starting transfers between devices, body(): parts = lax.all_to_all(packed, 'dp', 0, 0, tiled=True)  10.2 us
    all_to_all x1, starting transfers between devices, body(): lax.all_to_all(low_spread, 'tensor', 0, 0, tiled=True, axis_index_groups=...  10.1 us
    all_to_all x1, starting transfers between devices, body(): gathered = lax.all_to_all(spread, 'dp', 0, 0, tiled=True)  7.34 us
    pallas_call x1, Pallas kernels, body(): pl.pallas_call(base_kernel, grid=(2,), in_specs=[pl.BlockSpec(memory_spac...  4.58 us
    all_to_all x1, waiting for transfers between devices, body(): lax.all_to_all(low_spread, 'tensor', 0, 0, tiled=True, axis_index_groups=...  3.98 us
    all_gather x1, blocking collectives, body(): factors = lax.all_gather(gathered, 'tensor', axis_index_groups=pairs)  3.97 us
  transfers between devices with their start and end apart: 7, of which 3 were waited for; matrix products, arithmetic and copies ran while one was open for 0% of the time, Pallas kernels for 10%

profile of v7, /device:TPU:1, one launch (start us, length us, event | category | flops | bytes accessed | tf_op | source)
XLA Modules:
  0.0 83.2 jit_solution(15796161189745835145)
XLA Ops:
  0.6 0.0 copy-start.1
  0.6 0.0 copy-start.2
  0.7 0.0 copy-start.3
  0.7 0.0 copy-start.4
  0.7 1.8 %shard_map.121.after = bf16[16,48,128]{2,1,0:T(8,128)(2,1)} custom-call(f32[1,512,128]{2,1,0:T(8,128)} %grad_a.1, f32[1,32,384]{2,1,0:T(8,128)} %bitcast.9), custom_call_target="tpu_custom_call" | custom-call | tf_op jit(solution)/shard_map/pallas_call | solution.py:180
  2.5 10.2 %all-to-all-start = ((bf16[16,48,128]{2,1,0:T(8,128)(2,1)}), bf16[16,48,128]{2,1,0:T(8,128)(2,1)S(1)}, u32[]{:S(2)}, u32[]{:S(2)}) async-start(bf16[16,48,128]{2,1,0:T(8,128)(2,1)} %shard_map.121.after), calls=%async_computation | async-start | bytes 393216 | tf_op jit(solution)/shard_map/all_to_all | solution.py:184
  12.7 4.6 %shard_map.122 = (bf16[4,256,512]{2,1,0:T(8,128)(2,1)}, bf16[4,256,512]{2,1,0:T(8,128)(2,1)}, bf16[384,256]{1,0:T(8,128)(2,1)}, f32[8,256]{1,0:T(8,128)}) custom-call(bf16[16,48,128]{2,1,0:T(8,128)(2,1)} %shard_map.121.after, s32[8,256]{1,0:T(8,128)} %bitcast.10, f32[8,256]{1,0:T(8,128)} %bitcast.11, bf16[192,384]{1,0:T(8,128)(2,1)} %hidden.1, ...), custom_call_target="tpu_custom_call" | custom-call | flops 805306368 | bytes 7340032 | tf_op jit(solution)/shard_map/pallas_call | solution.py:185
  17.3 0.0 copy-start
  17.3 0.0 copy-start.6
  17.3 3.0 %collective-permute-start = (bf16[4,256,512]{2,1,0:T(8,128)(2,1)}, bf16[4,256,512]{2,1,0:T(8,128)(2,1)S(1)}, u32[]{:S(2)}, u32[]{:S(2)}) collective-permute-start(bf16[4,256,512]{2,1,0:T(8,128)(2,1)} %get-tuple-element.22), channel_id=1, source_target_pairs={{0,1},{1,0},{2,3},{3,2},{4,5},{5,4},{6,7},{7,6},{8,9},{9,8},{10,11... | collective-permute-start | bytes 3145736 | tf_op jit(solution)/shard_map/ppermute | solution.py:167
  20.3 2.0 %all-to-all-done.parts = bf16[16,48,128]{2,1,0:T(8,128)(2,1)S(1)} async-done(((bf16[16,48,128]{2,1,0:T(8,128)(2,1)}), bf16[16,48,128]{2,1,0:T(8,128)(2,1)S(1)}, u32[]{:S(2)}, u32[]{:S(2)}) %all-to-all-start) | async-done | bytes 196640 | tf_op jit(solution)/shard_map/all_to_all | solution.py:184
  22.4 0.0 copy-done.1
  22.4 0.0 copy-done.2
  22.4 0.0 copy-done.3
  22.4 0.0 copy-done.4
  22.4 0.8 %shard_map.124 = (f32[32,128]{1,0:T(8,128)S(1)}, f32[24,32]{1,0:T(8,128)S(1)}, bf16[16,48,128]{2,1,0:T(8,128)(2,1)}) custom-call(bf16[16,48,128]{2,1,0:T(8,128)(2,1)S(1)} %all-to-all-done.parts, f32[32,128]{1,0:T(8,128)S(1)} %copy-done.1, f32[32,128]{1,0:T(8,128)S(1)} %copy-done.2, f32[24,32]{1,0:T(8,128)S(1)} %copy-done.3, f32[24,32]{1,0:T(8,128)S(1)} %copy-done.4), custom_call_target="tpu_custom_call" | custom-call | flops 17179869184 | bytes 262144 | tf_op jit(solution)/shard_map/pallas_call | solution.py:206
  23.2 7.3 %all-to-all-start.1 = ((bf16[16,48,128]{2,1,0:T(8,128)(2,1)}), bf16[16,48,128]{2,1,0:T(8,128)(2,1)S(1)}, u32[]{:S(2)}, u32[]{:S(2)}) async-start(bf16[16,48,128]{2,1,0:T(8,128)(2,1)} %get-tuple-element.24), calls=%async_computation.1 | async-start | bytes 393216 | tf_op jit(solution)/shard_map/all_to_all | solution.py:216
  30.6 0.0 collective-permute-done.other
  30.6 0.0 copy-done
  30.6 0.8 %shard_map.123 = (bf16[256,512]{1,0:T(8,128)(2,1)S(1)}, bf16[256,512]{1,0:T(8,128)(2,1)S(1)}, bf16[256,512]{1,0:T(8,128)(2,1)}, f32[256,512]{1,0:T(8,128)S(1)}) custom-call(bf16[4,256,512]{2,1,0:T(8,128)(2,1)S(1)} %copy-done, bf16[4,256,512]{2,1,0:T(8,128)(2,1)S(1)} %collective-permute-done.other), custom_call_target="tpu_custom_call" | custom-call | flops 1048576 | bytes 4194304 | tf_op jit(solution)/shard_map/pallas_call | solution.py:218
  31.4 4.1 %collective-permute-start.1 = (bf16[256,512]{1,0:T(8,128)(2,1)}, bf16[256,512]{1,0:T(8,128)(2,1)S(1)}, u32[]{:S(2)}, u32[]{:S(2)}) collective-permute-start(bf16[256,512]{1,0:T(8,128)(2,1)} %get-tuple-element.36), channel_id=1, source_target_pairs={{0,6},{1,7},{2,4},{3,5},{4,2},{5,3},{6,0},{7,1},{8,14},{9,15},{10,... | collective-permute-start | bytes 786440 | tf_op jit(solution)/shard_map/ppermute | solution.py:167
  35.5 1.9 %collective-permute-start.2 = (bf16[256,512]{1,0:T(8,128)(2,1)S(1)}, bf16[256,512]{1,0:T(8,128)(2,1)S(1)}, u32[]{:S(2)}, u32[]{:S(2)}) collective-permute-start(bf16[256,512]{1,0:T(8,128)(2,1)S(1)} %get-tuple-element.37), channel_id=1, source_target_pairs={{0,4},{1,5},{2,6},{3,7},{4,0},{5,1},{6,2},{7,3},{8,12},{9,13},{10,... | collective-permute-start | bytes 786440 | tf_op jit(solution)/shard_map/ppermute | solution.py:167
  37.5 3.0 %collective-permute-start.3 = (bf16[256,512]{1,0:T(8,128)(2,1)S(1)}, bf16[256,512]{1,0:T(8,128)(2,1)S(1)}, u32[]{:S(2)}, u32[]{:S(2)}) collective-permute-start(bf16[256,512]{1,0:T(8,128)(2,1)S(1)} %get-tuple-element.38), channel_id=1, source_target_pairs={{0,2},{1,3},{2,0},{3,1},{4,6},{5,7},{6,4},{7,5},{8,10},{9,11},{10,... | collective-permute-start | bytes 786440 | tf_op jit(solution)/shard_map/ppermute | solution.py:167
  40.4 0.5 all-to-all-done.1.gathered
  40.9 0.0 copy-done.6
  40.9 0.0 copy-start.5
  40.9 0.9 %copy-done.5 = bf16[384,256]{1,0:T(8,128)(2,1)S(1)} copy-done((bf16[384,256]{1,0:T(8,128)(2,1)S(1)}, bf16[384,256]{1,0:T(8,128)(2,1)}, u32[]{:S(2)}) %copy-start.5) | copy-done | bytes 196632
  41.9 1.0 %shard_map.125 = bf16[16,32,256]{2,1,0:T(8,128)(2,1)} custom-call(bf16[16,48,128]{2,1,0:T(8,128)(2,1)S(1)} %all-to-all-done.1.gathered, bf16[384,256]{1,0:T(8,128)(2,1)S(1)} %copy-done.5, f32[8,256]{1,0:T(8,128)S(1)} %copy-done.6), custom_call_target="tpu_custom_call" | custom-call | flops 17179869184 | bytes 262144 | tf_op jit(solution)/shard_map/pallas_call | solution.py:225
  42.9 10.1 %all-to-all-start.2 = ((bf16[16,32,256]{2,1,0:T(8,128)(2,1)}), bf16[16,32,256]{2,1,0:T(8,128)(2,1)S(1)}, u32[]{:S(2)}, u32[]{:S(2)}) async-start(bf16[16,32,256]{2,1,0:T(8,128)(2,1)} %shard_map.125), calls=%async_computation.2 | async-start | bytes 524288 | tf_op jit(solution)/shard_map/all_to_all | solution.py:238
  53.0 0.6 shard_map.126
  53.6 4.0 %all-gather = bf16[32,48,128]{2,1,0:T(8,128)(2,1)S(1)} all-gather(bf16[16,48,128]{2,1,0:T(8,128)(2,1)S(1)} %all-to-all-done.1.gathered), channel_id=2, replica_groups={{0,1},{2,3},{4,5},{6,7},{8,9},{10,11},{12,13},{14,15},{16,17},{18,19},{..., dimensions={0}, use_global_device_ids=true | all-gather | bytes 589824 | tf_op jit(solution)/shard_map/all_gather | solution.py:239
  57.6 0.0 collective-permute-done.1.other_1
  57.6 0.0 collective-permute-done.2.other_2
  57.6 0.0 collective-permute-done.3.other_3
  57.6 0.1 shard_map.127.base
  57.7 4.0 %all-to-all-done.2 = bf16[16,32,256]{2,1,0:T(8,128)(2,1)S(1)} async-done(((bf16[16,32,256]{2,1,0:T(8,128)(2,1)}), bf16[16,32,256]{2,1,0:T(8,128)(2,1)S(1)}, u32[]{:S(2)}, u32[]{:S(2)}) %all-to-all-start.2) | async-done | bytes 262176 | tf_op jit(solution)/shard_map/all_to_all | solution.py:238
  61.7 0.3 shard_map.128
  62.0 20.5 %all_to_all.20.parts = bf16[32,8,768]{2,1,0:T(8,128)(2,1)S(1)} all-to-all(bf16[32,8,768]{2,1,0:T(8,128)(2,1)S(1)} %bitcast.7), channel_id=1, replica_groups=mesh['dp'=16,'tensor'=32] {'tensor'}, dimensions={0} | all-to-all | bytes 786432 | tf_op jit(solution)/shard_map/all_to_all | solution.py:252
  82.5 0.7 shard_map.129
Async XLA Ops:
  0.6 21.7 %copy-start.1 = (f32[32,128]{1,0:T(8,128)S(1)}, f32[32,128]{1,0:T(8,128)}, u32[]{:S(2)}) copy-start(f32[32,128]{1,0:T(8,128)} %factor_a.3) | copy-start | bytes 49156
  0.6 21.7 %copy-start.2 = (f32[32,128]{1,0:T(8,128)S(1)}, f32[32,128]{1,0:T(8,128)}, u32[]{:S(2)}) copy-start(f32[32,128]{1,0:T(8,128)} %moment_a.3) | copy-start | bytes 49156
  0.7 21.7 %copy-start.3 = (f32[24,32]{1,0:T(8,128)S(1)}, f32[24,32]{1,0:T(8,128)}, u32[]{:S(2)}) copy-start(f32[24,32]{1,0:T(8,128)} %factor_b.3) | copy-start | bytes 9220
  0.7 21.7 %copy-start.4 = (f32[24,32]{1,0:T(8,128)S(1)}, f32[24,32]{1,0:T(8,128)}, u32[]{:S(2)}) copy-start(f32[24,32]{1,0:T(8,128)} %moment_b.3) | copy-start | bytes 9220
  2.5 19.9 %all-to-all-start = ((bf16[16,48,128]{2,1,0:T(8,128)(2,1)}), bf16[16,48,128]{2,1,0:T(8,128)(2,1)S(1)}, u32[]{:S(2)}, u32[]{:S(2)}) async-start(bf16[16,48,128]{2,1,0:T(8,128)(2,1)} %shard_map.121.after), calls=%async_computation | async-start | bytes 393216 | tf_op jit(solution)/shard_map/all_to_all | solution.py:184
  17.3 13.3 %copy-start = (bf16[4,256,512]{2,1,0:T(8,128)(2,1)S(1)}, bf16[4,256,512]{2,1,0:T(8,128)(2,1)}, u32[]{:S(2)}) copy-start(bf16[4,256,512]{2,1,0:T(8,128)(2,1)} %get-tuple-element.21.own) | copy-start | bytes 3145732
  17.3 23.6 %copy-start.6 = (f32[8,256]{1,0:T(8,128)S(1)}, f32[8,256]{1,0:T(8,128)}, u32[]{:S(2)}) copy-start(f32[8,256]{1,0:T(8,128)} %get-tuple-element.26.row_weights) | copy-start | bytes 24580
  17.3 13.3 %collective-permute-start = (bf16[4,256,512]{2,1,0:T(8,128)(2,1)}, bf16[4,256,512]{2,1,0:T(8,128)(2,1)S(1)}, u32[]{:S(2)}, u32[]{:S(2)}) collective-permute-start(bf16[4,256,512]{2,1,0:T(8,128)(2,1)} %get-tuple-element.22), channel_id=1, source_target_pairs={{0,1},{1,0},{2,3},{3,2},{4,5},{5,4},{6,7},{7,6},{8,9},{9,8},{10,11... | collective-permute-start | bytes 3145736 | tf_op jit(solution)/shard_map/ppermute | solution.py:167
  23.2 17.7 %all-to-all-start.1 = ((bf16[16,48,128]{2,1,0:T(8,128)(2,1)}), bf16[16,48,128]{2,1,0:T(8,128)(2,1)S(1)}, u32[]{:S(2)}, u32[]{:S(2)}) async-start(bf16[16,48,128]{2,1,0:T(8,128)(2,1)} %get-tuple-element.24), calls=%async_computation.1 | async-start | bytes 393216 | tf_op jit(solution)/shard_map/all_to_all | solution.py:216
  31.4 26.2 %collective-permute-start.1 = (bf16[256,512]{1,0:T(8,128)(2,1)}, bf16[256,512]{1,0:T(8,128)(2,1)S(1)}, u32[]{:S(2)}, u32[]{:S(2)}) collective-permute-start(bf16[256,512]{1,0:T(8,128)(2,1)} %get-tuple-element.36), channel_id=1, source_target_pairs={{0,6},{1,7},{2,4},{3,5},{4,2},{5,3},{6,0},{7,1},{8,14},{9,15},{10,... | collective-permute-start | bytes 786440 | tf_op jit(solution)/shard_map/ppermute | solution.py:167
  35.5 22.1 %collective-permute-start.2 = (bf16[256,512]{1,0:T(8,128)(2,1)S(1)}, bf16[256,512]{1,0:T(8,128)(2,1)S(1)}, u32[]{:S(2)}, u32[]{:S(2)}) collective-permute-start(bf16[256,512]{1,0:T(8,128)(2,1)S(1)} %get-tuple-element.37), channel_id=1, source_target_pairs={{0,4},{1,5},{2,6},{3,7},{4,0},{5,1},{6,2},{7,3},{8,12},{9,13},{10,... | collective-permute-start | bytes 786440 | tf_op jit(solution)/shard_map/ppermute | solution.py:167
  37.5 20.1 %collective-permute-start.3 = (bf16[256,512]{1,0:T(8,128)(2,1)S(1)}, bf16[256,512]{1,0:T(8,128)(2,1)S(1)}, u32[]{:S(2)}, u32[]{:S(2)}) collective-permute-start(bf16[256,512]{1,0:T(8,128)(2,1)S(1)} %get-tuple-element.38), channel_id=1, source_target_pairs={{0,2},{1,3},{2,0},{3,1},{4,6},{5,7},{6,4},{7,5},{8,10},{9,11},{10,... | collective-permute-start | bytes 786440 | tf_op jit(solution)/shard_map/ppermute | solution.py:167
  40.9 0.9 %copy-start.5 = (bf16[384,256]{1,0:T(8,128)(2,1)S(1)}, bf16[384,256]{1,0:T(8,128)(2,1)}, u32[]{:S(2)}) copy-start(bf16[384,256]{1,0:T(8,128)(2,1)} %get-tuple-element.25.rows_t) | copy-start | bytes 589828
  42.9 18.9 %all-to-all-start.2 = ((bf16[16,32,256]{2,1,0:T(8,128)(2,1)}), bf16[16,32,256]{2,1,0:T(8,128)(2,1)S(1)}, u32[]{:S(2)}, u32[]{:S(2)}) async-start(bf16[16,32,256]{2,1,0:T(8,128)(2,1)} %shard_map.125), calls=%async_computation.2 | async-start | bytes 524288 | tf_op jit(solution)/shard_map/all_to_all | solution.py:238
